TPU v7x, 32 devices: a whole 2x2x4 slice. The times are simulated.
32 devices in a mesh: wide: 8 (over y, x, core), narrow: 4 (over z).
Axes of the slice: x: 2, y: 2, z: 4, core: 2. Of those that a mesh axis runs over, the one named last changes fastest.
Arguments:
- wavefunction: float32 [2, 512, 512, 256], P(None, 'wide', 'narrow'), may hold values from -6 to 6
- previous_slope: float32 [2, 512, 512, 256], P(None, 'wide', 'narrow'), may hold values from -6 to 6
- potential: float32 [512, 512, 256], P('wide', 'narrow'), may hold values from 0.5 to 3
- kinetic_one: float32 [512, 512], replicated, as said below
- coupling_one: float32 [512, 512], replicated, as said below
- kinetic_two: float32 [512, 512], P('narrow'), as said below
- coupling_two: float32 [512, 512], P('narrow'), as said below
- kinetic_three: float32 [256, 256], replicated, as said below
- coupling_three: float32 [256, 256], replicated, as said below
Outputs:
- slope: float32 [2, 512, 512, 256], P(None, 'wide', 'narrow')
- next_input: float32 [2, 512, 512, 256], P(None, 'wide', 'narrow')
Inputs may be any that keep to these rules, and one draw needn't show every extreme that they name: kinetic_one is symmetric. coupling_one is symmetric. kinetic_two is symmetric. coupling_two is symmetric. kinetic_three is symmetric. coupling_three is symmetric.
All inputs are finite; a program needn't handle non-finite values.
Results may differ from a plain program's by a relative error of at most 0.00005.
Values sent between devices are 32-bit elements; how exact they have to be, the bound alone decides.
A program may use at most 384 MiB of HBM per device.

v0:
```python
import jax
import jax.numpy as jnp
from jax import lax
from jax.sharding import PartitionSpec as P

half_step = 0.1
pieces = 2
HIGH = lax.Precision.HIGH


def along_one(matrix, field):
    return jnp.einsum("ij,jkl->ikl", matrix, field, precision=HIGH)


def along_two(matrix, field):
    return jnp.einsum("ij,kjl->kil", matrix, field, precision=HIGH)


def along_three(matrix, field):
    return jnp.einsum("ij,klj->kli", matrix, field, precision=HIGH)


def to_whole_one(field, wide):
    rows, second, third = field.shape
    blocks = field.reshape(rows, wide, second // wide, third).transpose(1, 0, 2, 3)
    moved = lax.all_to_all(blocks, "wide", split_axis=0, concat_axis=0, tiled=True)
    return moved.reshape(wide * rows, second // wide, third)


def from_whole_one(field, wide):
    rows, second, third = field.shape
    blocks = field.reshape(wide, rows // wide, second, third)
    moved = lax.all_to_all(blocks, "wide", split_axis=0, concat_axis=0, tiled=True)
    return moved.transpose(1, 0, 2, 3).reshape(rows // wide, wide * second, third)


def two_weights(kinetic_two, coupling_two):
    me = lax.axis_index("narrow")
    size = kinetic_two.shape[0]
    hub = jnp.where((me == 1) | (me == 2), 1.0, 0.0)
    slots = (me, jnp.maximum(me - 1, 0), jnp.minimum(me + 1, 3), jnp.where(me == 1, 3, 0))
    result = []
    for matrix in (coupling_two, kinetic_two):
        ends = lax.ppermute(matrix, "narrow", [(0, 1), (3, 2)])
        for rows in (ends, matrix * hub):
            result.append(jnp.concatenate([lax.dynamic_slice_in_dim(rows, slot * size, size, 1) for slot in slots], axis=1))
    return result


def middle_terms(weights, section):
    me = lax.axis_index("narrow")
    lower = lax.ppermute(section, "narrow", [(0, 1), (1, 2)])
    upper = lax.ppermute(section, "narrow", [(3, 2), (2, 1)])
    far = lax.ppermute(jnp.where(me == 1, lower, upper), "narrow", [(1, 2), (2, 1)])
    field = jnp.concatenate([section, lower, upper, far], axis=1)
    coupling_ends, coupling_own, kinetic_ends, kinetic_own = weights
    result = []
    for ends, own in ((coupling_ends, coupling_own), (kinetic_ends, kinetic_own)):
        received = lax.ppermute(along_two(ends, field), "narrow", [(1, 0), (2, 3)])
        result.append(along_two(own, field) + received)
    return result


def local(
    wide,
    wavefunction,
    previous_slope,
    potential,
    kinetic_one,
    coupling_one,
    kinetic_two,
    coupling_two,
    kinetic_three,
    coupling_three,
):
    rows = wavefunction.shape[1]
    half = rows // pieces
    sections = [wavefunction[c] + half_step * previous_slope[c] for c in range(2)]
    weights = two_weights(kinetic_two, coupling_two)
    second = [[middle_terms(weights, s[p * half:(p + 1) * half]) for p in range(pieces)] for s in sections]
    whole = [to_whole_one(s, wide) for s in sections]
    kinetic = [along_one(kinetic_one, s) for s in whole]
    base = [along_three(kinetic_three, s) + potential * s for s in sections]
    hamil = []
    for c in range(2):
        coupled = jnp.concatenate([along_three(coupling_three, terms[0]) for terms in second[c]])
        summed = kinetic[c] + along_one(coupling_one, to_whole_one(coupled, wide))
        middle = jnp.concatenate([terms[1] for terms in second[c]])
        hamil.append(from_whole_one(summed, wide) + middle + base[c])
    slope = jnp.stack([hamil[1], -hamil[0]])
    next_input = wavefunction + half_step * slope
    return (slope, next_input)


def solution(mesh):
    wide = mesh.shape["wide"]
    in_specs = (
        P(None, "wide", "narrow", None),
        P(None, "wide", "narrow", None),
        P("wide", "narrow", None),
        P(),
        P(),
        P("narrow", None),
        P("narrow", None),
        P(),
        P(),
    )
    out_specs = (P(None, "wide", "narrow", None), P(None, "wide", "narrow", None))

    def body(*arrays):
        return local(wide, *arrays)

    return jax.shard_map(body, mesh=mesh, in_specs=in_specs, out_specs=out_specs, check_vma=False)
```

profile of v0, /device:TPU:1, one launch (start us, length us, event | category | flops | bytes accessed | tf_op | source)
XLA Modules:
  0.0 1543.5 jit_solution(15128099692350465393)
XLA Ops:
  29.8 17.4 %copy.59 = f32[2,64,128,256]{2,3,1,0:T(8,128)} copy(f32[2,64,128,256]{3,2,1,0:T(8,128)} %param.9) | data formatting | bytes 33554432 | tf_op args[0]
  47.3 19.3 %slice_add_fusion.1 = (f32[1,64,128,256]{2,3,1,0:T(8,128)}, f32[1,64,128,256]{2,3,1,0:T(8,128)}) fusion(f32[2,64,128,256]{2,3,1,0:T(8,128)} %copy.59, f32[1,64,128,256]{2,3,1,0:T(8,128)} %copy.100, f32[1,64,128,256]{2,3,1,0:T(8,128)} %copy.101), kind=kLoop, calls=%fused_computation.7 | loop fusion | flops 8388608 | bytes 50331648 | tf_op jit(solution)/shard_map/add | solution.py:78
  112.0 55.9 %collective-permute-done = f32[32,128,256]{1,2,0:T(8,128)} collective-permute-done((f32[32,128,256]{1,2,0:T(8,128)}, f32[32,128,256]{1,2,0:T(8,128)}, u32[]{:S(2)}, u32[]{:S(2)}) %collective-permute-start) | collective-permute-done | bytes 4194336 | tf_op jit(solution)/shard_map/ppermute | solution.py:52
  171.8 86.0 %collective-permute-done.5 = f32[32,128,256]{1,2,0:T(8,128)} collective-permute-done((f32[32,128,256]{1,2,0:T(8,128)}, f32[32,128,256]{1,2,0:T(8,128)}, u32[]{:S(2)}, u32[]{:S(2)}) %collective-permute-start.5) | collective-permute-done | bytes 4194336 | tf_op jit(solution)/shard_map/ppermute | solution.py:52
  282.1 87.1 %collective-permute-done.3 = f32[128,512]{1,0:T(8,128)S(1)} collective-permute-done((f32[128,512]{1,0:T(8,128)S(1)}, f32[128,512]{1,0:T(8,128)S(1)}, u32[]{:S(2)}, u32[]{:S(2)}) %collective-permute-start.3) | collective-permute-done | bytes 262176 | tf_op jit(solution)/shard_map/ppermute | solution.py:44
  414.2 11.7 convolution_bitcast_fusion.7
  427.1 11.7 convolution_bitcast_fusion.6
  448.0 18.8 %collective-permute-done.16 = f32[32,128,256]{1,2,0:T(8,128)} collective-permute-done((f32[32,128,256]{1,2,0:T(8,128)}, f32[32,128,256]{1,2,0:T(8,128)}, u32[]{:S(2)}, u32[]{:S(2)}) %collective-permute-start.16) | collective-permute-done | bytes 4194336 | tf_op jit(solution)/shard_map/ppermute | solution.py:52
  494.9 36.9 %collective-permute-done.4 = f32[32,128,256]{1,2,0:T(8,128)} collective-permute-done((f32[32,128,256]{1,2,0:T(8,128)}, f32[32,128,256]{1,2,0:T(8,128)}, u32[]{:S(2)}, u32[]{:S(2)}) %collective-permute-start.4) | collective-permute-done | bytes 4194336 | tf_op jit(solution)/shard_map/ppermute | solution.py:59
  537.4 84.2 %collective-permute-done.8 = f32[32,128,256]{1,2,0:T(8,128)} collective-permute-done((f32[32,128,256]{1,2,0:T(8,128)}, f32[32,128,256]{1,2,0:T(8,128)}, u32[]{:S(2)}, u32[]{:S(2)}) %collective-permute-start.8) | collective-permute-done | bytes 4194336 | tf_op jit(solution)/shard_map/ppermute | solution.py:59
  657.8 11.7 convolution_bitcast_fusion.2
  691.7 119.9 %collective-permute-done.15 = f32[32,128,256]{1,2,0:T(8,128)S(1)} collective-permute-done((f32[32,128,256]{1,2,0:T(8,128)S(1)}, f32[32,128,256]{1,2,0:T(8,128)S(1)}, u32[]{:S(2)}, u32[]{:S(2)}) %collective-permute-start.15) | collective-permute-done | bytes 4194336 | tf_op jit(solution)/shard_map/ppermute | solution.py:59
  815.1 89.3 %collective-permute-done.19 = f32[32,128,256]{1,2,0:T(8,128)S(1)} collective-permute-done((f32[32,128,256]{1,2,0:T(8,128)}, f32[32,128,256]{1,2,0:T(8,128)S(1)}, u32[]{:S(2)}, u32[]{:S(2)}) %collective-permute-start.19) | collective-permute-done | bytes 4194336 | tf_op jit(solution)/shard_map/ppermute | solution.py:59
  925.2 17.9 %fusion.15 = f32[16,256,512]{2,1,0:T(8,128)S(1)} fusion(f32[512,16,256]{2,1,0:T(8,128)} %bitcast.15, f32[512,512]{1,0:T(8,128)S(1)} %copy-done), kind=kOutput, calls=%fused_computation.30 | convolution fusion | flops 6442450944 | bytes 17825792 | tf_op jit(solution)/shard_map/ij,jkl->ikl/dot_general | solution.py:12
  943.1 20.2 %add_bitcast_fusion.1 = f32[512,16,256]{0,2,1:T(8,128)} fusion(f32[16,256,512]{2,1,0:T(8,128)S(1)} %fusion.15, f32[512,16,256]{2,1,0:T(8,128)} %bitcast.2, f32[512,512]{1,0:T(8,128)S(1)} %copy-done.3), kind=kOutput, calls=%fused_computation.36 | convolution fusion | flops 6444548096 | bytes 26214400 | tf_op jit(solution)/shard_map/ij,jkl->ikl/dot_general | solution.py:12
  973.6 42.1 %all-to-all-done.4 = f32[8,64,16,256]{3,2,1,0:T(8,128)} async-done(((f32[8,64,16,256]{3,2,1,0:T(8,128)}), f32[8,64,16,256]{3,2,1,0:T(8,128)}, u32[]{:S(2)}, u32[]{:S(2)}) %all-to-all-start.4) | async-done | bytes 8388640 | tf_op jit(solution)/shard_map/all_to_all | solution.py:26
  1033.5 11.7 convolution_bitcast_fusion.5
  1046.5 17.8 %fusion.11 = f32[16,256,512]{2,1,0:T(8,128)S(1)} fusion(f32[512,16,256]{2,1,0:T(8,128)} %bitcast.41, f32[512,512]{1,0:T(8,128)S(1)} %copy-done), kind=kOutput, calls=%fused_computation.25 | convolution fusion | flops 6442450944 | bytes 17825792 | tf_op jit(solution)/shard_map/ij,jkl->ikl/dot_general | solution.py:12
  1064.4 20.0 %add_bitcast_fusion = f32[512,16,256]{0,2,1:T(8,128)} fusion(f32[16,256,512]{2,1,0:T(8,128)S(1)} %fusion.11, f32[512,16,256]{2,1,0:T(8,128)} %bitcast.32, f32[512,512]{1,0:T(8,128)S(1)} %copy-done.3), kind=kOutput, calls=%fused_computation.35 | convolution fusion | flops 6444548096 | bytes 26214400 | tf_op jit(solution)/shard_map/ij,jkl->ikl/dot_general | solution.py:12
  1094.6 20.2 %all-to-all-done.2 = f32[8,64,16,256]{3,2,1,0:T(8,128)} async-done(((f32[8,64,16,256]{3,2,1,0:T(8,128)}), f32[8,64,16,256]{3,2,1,0:T(8,128)}, u32[]{:S(2)}, u32[]{:S(2)}) %all-to-all-start.2) | async-done | bytes 8388640 | tf_op jit(solution)/shard_map/all_to_all | solution.py:33
  1123.8 11.7 convolution_bitcast_fusion.4
  1136.8 11.7 convolution_bitcast_fusion.1
  1150.0 11.7 convolution_bitcast_fusion
  1163.1 11.3 fusion.44
  1211.7 18.0 %collective-permute-done.11 = f32[32,128,256]{1,2,0:T(8,128)S(1)} collective-permute-done((f32[32,128,256]{1,2,0:T(8,128)}, f32[32,128,256]{1,2,0:T(8,128)S(1)}, u32[]{:S(2)}, u32[]{:S(2)}) %collective-permute-start.11) | collective-permute-done | bytes 4194336 | tf_op jit(solution)/shard_map/ppermute | solution.py:59
  1232.3 87.3 %collective-permute-done.20 = f32[32,128,256]{1,2,0:T(8,128)S(1)} collective-permute-done((f32[32,128,256]{1,2,0:T(8,128)}, f32[32,128,256]{1,2,0:T(8,128)S(1)}, u32[]{:S(2)}, u32[]{:S(2)}) %collective-permute-start.20) | collective-permute-done | bytes 4194336 | tf_op jit(solution)/shard_map/ppermute | solution.py:59
  1322.3 87.2 %collective-permute-done.21 = f32[32,128,256]{1,2,0:T(8,128)S(1)} collective-permute-done((f32[32,128,256]{1,2,0:T(8,128)}, f32[32,128,256]{1,2,0:T(8,128)S(1)}, u32[]{:S(2)}, u32[]{:S(2)}) %collective-permute-start.21) | collective-permute-done | bytes 4194336 | tf_op jit(solution)/shard_map/ppermute | solution.py:59
  1446.4 21.0 %fusion.1 = f32[1,64,128,256]{2,3,1,0:T(8,128)} fusion(f32[64,128,256]{1,2,0:T(8,128)} %copy.70, f32[32,128,256]{1,2,0:T(8,128)} %bitcast_add_fusion.6, f32[32,128,256]{1,2,0:T(8,128)} %bitcast_add_fusion.7, f32[64,128,256]{1,2,0:T(8,128)} %copy.72, f32[1,64,128,256]{2,3,1,0:T(8,128)} %get-tuple-element.10, f32[256,256]{1,0:T(8,128)S(1)} %copy-done.5), kind=kOutput, calls=%fused_computation.11 | convolution fusion | flops 3231711232 | bytes 42205184 | tf_op jit(solution)/shard_map/ij,klj->kli/dot_general | solution.py:20
  1467.5 19.6 %fusion.4 = f32[1,64,128,256]{2,3,1,0:T(8,128)} fusion(f32[64,128,256]{1,2,0:T(8,128)} %copy.85, f32[32,128,256]{1,2,0:T(8,128)} %bitcast_add_fusion, f32[32,128,256]{1,2,0:T(8,128)S(1)} %copy-done.2, f32[64,128,256]{1,2,0:T(8,128)} %copy.72, f32[1,64,128,256]{2,3,1,0:T(8,128)} %get-tuple-element.11, f32[256,256]{1,0:T(8,128)S(1)} %copy-done.5), kind=kOutput, calls=%fused_computation.16 | convolution fusion | flops 3233808384 | bytes 42205184 | tf_op jit(solution)/shard_map/ij,klj->kli/dot_general | solution.py:20
  1487.1 21.1 %multiply_add_fusion = (f32[2,64,128,256]{2,3,1,0:T(8,128)}, f32[2,64,128,256]{2,3,1,0:T(8,128)}) fusion(f32[2,64,128,256]{2,3,1,0:T(8,128)} %copy.59, f32[1,64,128,256]{2,3,1,0:T(8,128)} %fusion.4, f32[1,64,128,256]{2,3,1,0:T(8,128)} %fusion.1), kind=kLoop, calls=%fused_computation.5 | loop fusion | flops 12582912 | bytes 67108864 | tf_op jit(solution)/shard_map/add | solution.py:91
  1508.2 17.5 %copy.90 = f32[2,64,128,256]{3,2,1,0:T(8,128)} copy(f32[2,64,128,256]{2,3,1,0:T(8,128)} %get-tuple-element.9) | data formatting | bytes 33554432
  1525.7 17.6 %copy.91 = f32[2,64,128,256]{3,2,1,0:T(8,128)} copy(f32[2,64,128,256]{2,3,1,0:T(8,128)} %get-tuple-element.8) | data formatting | bytes 33554432
  (121 shorter events, 406.5 us)
Async XLA Ops:
  0.6 924.5 %copy-start = (f32[512,512]{1,0:T(8,128)S(1)}, f32[512,512]{1,0:T(8,128)}, u32[]{:S(2)}) copy-start(f32[512,512]{1,0:T(8,128)} %param.13) | copy-start | bytes 3145732
  74.3 93.6 %collective-permute-start = (f32[32,128,256]{1,2,0:T(8,128)}, f32[32,128,256]{1,2,0:T(8,128)}, u32[]{:S(2)}, u32[]{:S(2)}) collective-permute-start(f32[32,128,256]{1,2,0:T(8,128)} %get-tuple-element.14), channel_id=1, source_target_pairs={{0,1},{1,2},{4,5},{5,6},{8,9},{9,10},{12,13},{13,14},{16,17},{17,1... | collective-permute-start | bytes 12582920 | tf_op jit(solution)/shard_map/ppermute | solution.py:52
  80.5 87.4 %collective-permute-start.1 = (f32[32,128,256]{1,2,0:T(8,128)}, f32[32,128,256]{1,2,0:T(8,128)}, u32[]{:S(2)}, u32[]{:S(2)}) collective-permute-start(f32[32,128,256]{1,2,0:T(8,128)} %get-tuple-element.14), channel_id=1, source_target_pairs={{3,2},{2,1},{7,6},{6,5},{11,10},{10,9},{15,14},{14,13},{19,18},{18... | collective-permute-start | bytes 12582920 | tf_op jit(solution)/shard_map/ppermute | solution.py:53
  83.1 174.7 %collective-permute-start.5 = (f32[32,128,256]{1,2,0:T(8,128)}, f32[32,128,256]{1,2,0:T(8,128)}, u32[]{:S(2)}, u32[]{:S(2)}) collective-permute-start(f32[32,128,256]{1,2,0:T(8,128)} %get-tuple-element.15), channel_id=1, source_target_pairs={{0,1},{1,2},{4,5},{5,6},{8,9},{9,10},{12,13},{13,14},{16,17},{17,1... | collective-permute-start | bytes 12582920 | tf_op jit(solution)/shard_map/ppermute | solution.py:52
  86.4 171.4 %collective-permute-start.6 = (f32[32,128,256]{1,2,0:T(8,128)}, f32[32,128,256]{1,2,0:T(8,128)}, u32[]{:S(2)}, u32[]{:S(2)}) collective-permute-start(f32[32,128,256]{1,2,0:T(8,128)} %get-tuple-element.15), channel_id=1, source_target_pairs={{3,2},{2,1},{7,6},{6,5},{11,10},{10,9},{15,14},{14,13},{19,18},{18... | collective-permute-start | bytes 12582920 | tf_op jit(solution)/shard_map/ppermute | solution.py:53
  106.2 298.3 %all-to-all-start = ((f32[8,64,16,256]{3,2,1,0:T(8,128)}), f32[8,64,16,256]{3,2,1,0:T(8,128)}, u32[]{:S(2)}, u32[]{:S(2)}) async-start(f32[8,64,16,256]{3,2,1,0:T(8,128)} %copy.62), calls=%async_computation | async-start | bytes 16777216 | tf_op jit(solution)/shard_map/all_to_all | solution.py:26
  167.9 97.3 %slice-start = ((s8[8388608]{0:T(1024)(128)(4,1)}), s8[4194304]{0:T(1024)(128)(4,1)S(1)}, s32[]{:S(2)}) async-start(s8[8388608]{0:T(1024)(128)(4,1)} %bitcast.144), calls=%async_computation.6 | async-start | bytes 8388608
  170.8 94.5 %slice-start.1 = ((s8[8388608]{0:T(1024)(128)(4,1)}), s8[4194304]{0:T(1024)(128)(4,1)S(1)}, s32[]{:S(2)}) async-start(s8[8388608]{0:T(1024)(128)(4,1)} %bitcast.144), calls=%async_computation.7 | async-start | bytes 8388608
  170.8 212.1 %collective-permute-start.2 = (f32[32,128,256]{1,2,0:T(8,128)S(1)}, f32[32,128,256]{1,2,0:T(8,128)S(1)}, u32[]{:S(2)}, u32[]{:S(2)}) collective-permute-start(f32[32,128,256]{1,2,0:T(8,128)S(1)} %broadcast_select_fusion.3), channel_id=1, source_target_pairs={{1,2},{2,1},{5,6},{6,5},{9,10},{10,9},{13,14},{14,13},{17,18},{18,... | collective-permute-start | bytes 12582920 | tf_op jit(solution)/shard_map/ppermute | solution.py:54
  262.6 163.2 %collective-permute-start.7 = (f32[32,128,256]{1,2,0:T(8,128)}, f32[32,128,256]{1,2,0:T(8,128)}, u32[]{:S(2)}, u32[]{:S(2)}) collective-permute-start(f32[32,128,256]{1,2,0:T(8,128)} %broadcast_select_fusion.2), channel_id=1, source_target_pairs={{1,2},{2,1},{5,6},{6,5},{9,10},{10,9},{13,14},{14,13},{17,18},{18,... | collective-permute-start | bytes 12582920 | tf_op jit(solution)/shard_map/ppermute | solution.py:54
  265.3 103.9 %copy-start.7 = (f32[128,512]{1,0:T(8,128)S(1)}, f32[128,512]{1,0:T(8,128)}, u32[]{:S(2)}) copy-start(f32[128,512]{1,0:T(8,128)} %param.14) | copy-start | bytes 786436
  269.1 169.8 %collective-permute-start.12 = (f32[32,128,256]{1,2,0:T(8,128)}, f32[32,128,256]{1,2,0:T(8,128)}, u32[]{:S(2)}, u32[]{:S(2)}) collective-permute-start(f32[32,128,256]{1,2,0:T(8,128)} %get-tuple-element.16), channel_id=1, source_target_pairs={{0,1},{1,2},{4,5},{5,6},{8,9},{9,10},{12,13},{13,14},{16,17},{17,1... | collective-permute-start | bytes 12582920 | tf_op jit(solution)/shard_map/ppermute | solution.py:52
  278.1 162.1 %collective-permute-start.13 = (f32[32,128,256]{1,2,0:T(8,128)}, f32[32,128,256]{1,2,0:T(8,128)}, u32[]{:S(2)}, u32[]{:S(2)}) collective-permute-start(f32[32,128,256]{1,2,0:T(8,128)} %get-tuple-element.16), channel_id=1, source_target_pairs={{3,2},{2,1},{7,6},{6,5},{11,10},{10,9},{15,14},{14,13},{19,18},{18... | collective-permute-start | bytes 12582920 | tf_op jit(solution)/shard_map/ppermute | solution.py:53
  280.8 88.4 %collective-permute-start.3 = (f32[128,512]{1,0:T(8,128)S(1)}, f32[128,512]{1,0:T(8,128)S(1)}, u32[]{:S(2)}, u32[]{:S(2)}) collective-permute-start(f32[128,512]{1,0:T(8,128)S(1)} %copy-done.6), channel_id=1, source_target_pairs={{0,1},{3,2},{4,5},{7,6},{8,9},{11,10},{12,13},{15,14},{16,17},{19,... | collective-permute-start | bytes 786440 | tf_op jit(solution)/shard_map/ppermute | solution.py:44
  369.1 7.5 collective-permute-start.9
  376.7 90.2 %collective-permute-start.16 = (f32[32,128,256]{1,2,0:T(8,128)}, f32[32,128,256]{1,2,0:T(8,128)}, u32[]{:S(2)}, u32[]{:S(2)}) collective-permute-start(f32[32,128,256]{1,2,0:T(8,128)} %get-tuple-element.17), channel_id=1, source_target_pairs={{0,1},{1,2},{4,5},{5,6},{8,9},{9,10},{12,13},{13,14},{16,17},{17,1... | collective-permute-start | bytes 12582920 | tf_op jit(solution)/shard_map/ppermute | solution.py:52
  384.8 82.0 %collective-permute-start.17 = (f32[32,128,256]{1,2,0:T(8,128)}, f32[32,128,256]{1,2,0:T(8,128)}, u32[]{:S(2)}, u32[]{:S(2)}) collective-permute-start(f32[32,128,256]{1,2,0:T(8,128)} %get-tuple-element.17), channel_id=1, source_target_pairs={{3,2},{2,1},{7,6},{6,5},{11,10},{10,9},{15,14},{14,13},{19,18},{18... | collective-permute-start | bytes 12582920 | tf_op jit(solution)/shard_map/ppermute | solution.py:53
  404.5 232.3 %all-to-all-start.3 = ((f32[8,64,16,256]{3,2,1,0:T(8,128)}), f32[8,64,16,256]{3,2,1,0:T(8,128)}, u32[]{:S(2)}, u32[]{:S(2)}) async-start(f32[8,64,16,256]{3,2,1,0:T(8,128)} %copy.77), calls=%async_computation.3 | async-start | bytes 16777216 | tf_op jit(solution)/shard_map/all_to_all | solution.py:26
  425.9 105.9 %collective-permute-start.4 = (f32[32,128,256]{1,2,0:T(8,128)}, f32[32,128,256]{1,2,0:T(8,128)}, u32[]{:S(2)}, u32[]{:S(2)}) collective-permute-start(f32[32,128,256]{1,2,0:T(8,128)} %convolution_bitcast_fusion.7), channel_id=1, source_target_pairs={{1,0},{2,3},{5,4},{6,7},{9,8},{10,11},{13,12},{14,15},{17,16},{18,... | collective-permute-start | bytes 12582920 | tf_op jit(solution)/shard_map/ppermute | solution.py:59
  438.9 182.8 %collective-permute-start.8 = (f32[32,128,256]{1,2,0:T(8,128)}, f32[32,128,256]{1,2,0:T(8,128)}, u32[]{:S(2)}, u32[]{:S(2)}) collective-permute-start(f32[32,128,256]{1,2,0:T(8,128)} %convolution_bitcast_fusion.6), channel_id=1, source_target_pairs={{1,0},{2,3},{5,4},{6,7},{9,8},{10,11},{13,12},{14,15},{17,16},{18,... | collective-permute-start | bytes 12582920 | tf_op jit(solution)/shard_map/ppermute | solution.py:59
  445.2 200.4 %collective-permute-start.14 = (f32[32,128,256]{1,2,0:T(8,128)}, f32[32,128,256]{1,2,0:T(8,128)}, u32[]{:S(2)}, u32[]{:S(2)}) collective-permute-start(f32[32,128,256]{1,2,0:T(8,128)} %broadcast_select_fusion.1), channel_id=1, source_target_pairs={{1,2},{2,1},{5,6},{6,5},{9,10},{10,9},{13,14},{14,13},{17,18},{18,... | collective-permute-start | bytes 12582920 | tf_op jit(solution)/shard_map/ppermute | solution.py:54
  471.7 186.1 %collective-permute-start.18 = (f32[32,128,256]{1,2,0:T(8,128)}, f32[32,128,256]{1,2,0:T(8,128)}, u32[]{:S(2)}, u32[]{:S(2)}) collective-permute-start(f32[32,128,256]{1,2,0:T(8,128)} %broadcast_select_fusion), channel_id=1, source_target_pairs={{1,2},{2,1},{5,6},{6,5},{9,10},{10,9},{13,14},{14,13},{17,18},{18,... | collective-permute-start | bytes 12582920 | tf_op jit(solution)/shard_map/ppermute | solution.py:54
  636.8 280.7 %all-to-all-start.1 = ((f32[8,64,16,256]{3,2,1,0:T(8,128)}), f32[8,64,16,256]{3,2,1,0:T(8,128)}, u32[]{:S(2)}, u32[]{:S(2)}) async-start(f32[8,64,16,256]{3,2,1,0:T(8,128)} %bitcast.147), calls=%async_computation.1 | async-start | bytes 16777216 | tf_op jit(solution)/shard_map/all_to_all | solution.py:26
  656.0 155.6 %collective-permute-start.15 = (f32[32,128,256]{1,2,0:T(8,128)S(1)}, f32[32,128,256]{1,2,0:T(8,128)S(1)}, u32[]{:S(2)}, u32[]{:S(2)}) collective-permute-start(f32[32,128,256]{1,2,0:T(8,128)S(1)} %convolution_bitcast_fusion.3), channel_id=1, source_target_pairs={{1,0},{2,3},{5,4},{6,7},{9,8},{10,11},{13,12},{14,15},{17,16},{18,... | collective-permute-start | bytes 12582920 | tf_op jit(solution)/shard_map/ppermute | solution.py:59
  669.6 234.9 %collective-permute-start.19 = (f32[32,128,256]{1,2,0:T(8,128)}, f32[32,128,256]{1,2,0:T(8,128)S(1)}, u32[]{:S(2)}, u32[]{:S(2)}) collective-permute-start(f32[32,128,256]{1,2,0:T(8,128)} %convolution_bitcast_fusion.2), channel_id=1, source_target_pairs={{1,0},{2,3},{5,4},{6,7},{9,8},{10,11},{13,12},{14,15},{17,16},{18,... | collective-permute-start | bytes 12582920 | tf_op jit(solution)/shard_map/ppermute | solution.py:59
  917.5 98.1 %all-to-all-start.4 = ((f32[8,64,16,256]{3,2,1,0:T(8,128)}), f32[8,64,16,256]{3,2,1,0:T(8,128)}, u32[]{:S(2)}, u32[]{:S(2)}) async-start(f32[8,64,16,256]{3,2,1,0:T(8,128)} %bitcast.149), calls=%async_computation.4 | async-start | bytes 16777216 | tf_op jit(solution)/shard_map/all_to_all | solution.py:26
  1015.7 99.2 %all-to-all-start.2 = ((f32[8,64,16,256]{3,2,1,0:T(8,128)}), f32[8,64,16,256]{3,2,1,0:T(8,128)}, u32[]{:S(2)}, u32[]{:S(2)}) async-start(f32[8,64,16,256]{3,2,1,0:T(8,128)} %bitcast.148), calls=%async_computation.2 | async-start | bytes 16777216 | tf_op jit(solution)/shard_map/all_to_all | solution.py:33
  1045.3 160.3 %collective-permute-start.10 = (f32[32,128,256]{1,2,0:T(8,128)}, f32[32,128,256]{1,2,0:T(8,128)}, u32[]{:S(2)}, u32[]{:S(2)}) collective-permute-start(f32[32,128,256]{1,2,0:T(8,128)} %convolution_bitcast_fusion.5), channel_id=1, source_target_pairs={{1,0},{2,3},{5,4},{6,7},{9,8},{10,11},{13,12},{14,15},{17,16},{18,... | collective-permute-start | bytes 12582920 | tf_op jit(solution)/shard_map/ppermute | solution.py:59
  1114.9 314.4 %all-to-all-start.5 = ((f32[8,64,16,256]{3,2,1,0:T(8,128)}), f32[8,64,16,256]{3,2,1,0:T(8,128)}, u32[]{:S(2)}, u32[]{:S(2)}) async-start(f32[8,64,16,256]{3,2,1,0:T(8,128)} %bitcast.146), calls=%async_computation.5 | async-start | bytes 16777216 | tf_op jit(solution)/shard_map/all_to_all | solution.py:33
  1135.5 94.2 %collective-permute-start.11 = (f32[32,128,256]{1,2,0:T(8,128)}, f32[32,128,256]{1,2,0:T(8,128)S(1)}, u32[]{:S(2)}, u32[]{:S(2)}) collective-permute-start(f32[32,128,256]{1,2,0:T(8,128)} %convolution_bitcast_fusion.4), channel_id=1, source_target_pairs={{1,0},{2,3},{5,4},{6,7},{9,8},{10,11},{13,12},{14,15},{17,16},{18,... | collective-permute-start | bytes 12582920 | tf_op jit(solution)/shard_map/ppermute | solution.py:59
  1148.5 171.1 %collective-permute-start.20 = (f32[32,128,256]{1,2,0:T(8,128)}, f32[32,128,256]{1,2,0:T(8,128)S(1)}, u32[]{:S(2)}, u32[]{:S(2)}) collective-permute-start(f32[32,128,256]{1,2,0:T(8,128)} %convolution_bitcast_fusion.1), channel_id=1, source_target_pairs={{1,0},{2,3},{5,4},{6,7},{9,8},{10,11},{13,12},{14,15},{17,16},{18,... | collective-permute-start | bytes 12582920 | tf_op jit(solution)/shard_map/ppermute | solution.py:59
  1161.8 247.7 %collective-permute-start.21 = (f32[32,128,256]{1,2,0:T(8,128)}, f32[32,128,256]{1,2,0:T(8,128)S(1)}, u32[]{:S(2)}, u32[]{:S(2)}) collective-permute-start(f32[32,128,256]{1,2,0:T(8,128)} %convolution_bitcast_fusion), channel_id=1, source_target_pairs={{1,0},{2,3},{5,4},{6,7},{9,8},{10,11},{13,12},{14,15},{17,16},{18,... | collective-permute-start | bytes 12582920 | tf_op jit(solution)/shard_map/ppermute | solution.py:59
  (12 other events, 242.2 us)
where the time goes:
time: 1560 us; the launch traced here: 1540 us
  waiting for transfers between devices  836 us (54%)
  matrix products  315 us (20%)
  local copies, waits for them, and re-layouts  203 us (13%)
  starting transfers between devices  110 us (7%)
  other arithmetic  77.8 us (5%)
    ppermute x8, waiting for transfers between devices, middle_terms(): received = lax.ppermute(along_two(ends, field), 'narrow', [(1, 0), (2, 3)])  523 us
    dot_general x16, matrix products, along_two(): return jnp.einsum('ij,kjl->kil', matrix, field, precision=HIGH)  176 us
    ppermute x4, waiting for transfers between devices, middle_terms(): lower = lax.ppermute(section, 'narrow', [(0, 1), (1, 2)])  161 us
    ppermute x2, waiting for transfers between devices, two_weights(): ends = lax.ppermute(matrix, 'narrow', [(0, 1), (3, 2)])  90.4 us
    unnamed x38, local copies, waits for them, and re-layouts  81.7 us
    dot_general x4, matrix products, along_one(): return jnp.einsum('ij,jkl->ikl', matrix, field, precision=HIGH)  75.8 us
    dot_general x6, matrix products, along_three(): return jnp.einsum('ij,klj->kli', matrix, field, precision=HIGH)  62.9 us
    all_to_all x4, waiting for transfers between devices, to_whole_one(): lax.all_to_all(blocks, 'wide', split_axis=0, concat_axis=0, tiled=True)  42.1 us
  transfers between devices with their start and end apart: 28, of which 14 were waited for; matrix products, arithmetic and copies ran while one was open for 26% of the time, Pallas kernels for 0%

commit v1 on v0

v1 whole, which is shorter than its diff:
```python
import functools

import jax
import jax.numpy as jnp
from jax import lax
from jax.experimental import pallas as pl
from jax.experimental.pallas import tpu as pltpu
from jax.sharding import PartitionSpec as P

half_step = 0.1
MESH = pl.DeviceIdType.MESH
OWN, END, FWD, YROW, WROW, PSI, PHI, SUM_O, SUM_F, YEND = range(10)
TO_S1, BACK_C, BACK_K, TO_S0, TO_W0, BACK_0 = range(6)
BUFFERS = (
    "end0", "other0", "far0", "y0", "w0", "sy", "sw",
    "s0b", "t0", "w0b", "tw", "r0", "b0",
    "s1b", "t1", "rc", "rk", "bc", "bk", "phi",
    "psie", "phie", "po", "pe", "ao", "af", "ba0", "ba1", "se", "y1", "base1", "h0",
)
WIDE_SHAPED = ("t0", "tw", "r0", "t1", "rc", "rk")
SECOND_FIRST = ("s0b", "w0b", "b0", "s1b", "bc", "bk")


def halves(x):
    high = x.astype(jnp.bfloat16)
    return high, (x - high.astype(jnp.float32)).astype(jnp.bfloat16)


def dot3(ah, al, bh, bl):
    dot = functools.partial(jnp.dot, preferred_element_type=jnp.float32)
    return dot(ah, bh) + dot(ah, bl) + dot(al, bh)


def kernel(wide, s, pot, w, wt, k1, c1, k3, c3, *refs):
    buf = dict(zip(BUFFERS, refs[:len(BUFFERS)]))
    (wh, wl, wth, wtl, k1h, k1l, c1h, c1l, k3h, k3l, c3h, c3l, fh, fl, gather,
     zs, zr, ws, wr, wloc) = refs[len(BUFFERS):]
    rows, second, third = s.shape[1:]
    full = rows * wide
    q = second // wide
    step = 8
    nc = rows // step
    me = lax.axis_index("wide")
    z = lax.axis_index("narrow")
    hub = jnp.logical_or(z == 1, z == 2)
    end = jnp.where(z == 1, 0, 3)
    other = 3 - z
    far = 3 - end
    my_hub = jnp.where(z == 0, 1, 2)
    s0, s1 = s.at[0], s.at[1]

    def peer_of(d):
        return lax.rem(me + d, wide)

    barrier = pltpu.get_barrier_semaphore()

    def greet(d, carry):
        pl.semaphore_signal(barrier, inc=1, device_id={"wide": peer_of(d)}, device_id_type=MESH)
        return carry

    lax.fori_loop(1, wide, greet, 0)

    @pl.when(hub)
    def _():
        pl.semaphore_signal(barrier, inc=1, device_id={"narrow": end}, device_id_type=MESH)
        pl.semaphore_signal(barrier, inc=1, device_id={"narrow": other}, device_id_type=MESH)
        pl.semaphore_wait(barrier, wide + 1)

    @pl.when(jnp.logical_not(hub))
    def _():
        pl.semaphore_signal(barrier, inc=1, device_id={"narrow": my_hub}, device_id_type=MESH)
        pl.semaphore_wait(barrier, wide)

    def piece(ref, c):
        return ref.at[pl.ds(pl.multiple_of(c * step, step), step)]

    def zcopy(kind, c, src, dst, target):
        return pltpu.make_async_remote_copy(
            src_ref=piece(src, c), dst_ref=piece(dst, c), send_sem=zs.at[kind, c], recv_sem=zr.at[kind, c],
            device_id={"narrow": target}, device_id_type=MESH)

    def zrecv(kind, c, dst):
        pltpu.make_async_copy(piece(dst, c), piece(dst, c), zr.at[kind, c]).wait()

    def zsent(kind, c, src):
        pltpu.make_async_copy(piece(src, c), piece(src, c), zs.at[kind, c]).wait()

    def each_chunk(f):
        def body(c, carry):
            f(c)
            return carry
        lax.fori_loop(0, nc, body, 0)

    def mine_of(ref, index, size):
        return ref.at[:, pl.ds(pl.multiple_of(index * size, size), size)]

    def to_whole(kind, src, dst):
        def send(d, carry):
            p = peer_of(d)
            pltpu.make_async_remote_copy(
                src_ref=src.at[pl.ds(p * q, q)], dst_ref=mine_of(dst, me, rows),
                send_sem=ws.at[kind], recv_sem=wr.at[kind], device_id={"wide": p}, device_id_type=MESH).start()
            return carry
        lax.fori_loop(1, wide, send, 0)
        pltpu.make_async_copy(src.at[pl.ds(me * q, q)], mine_of(dst, me, rows), wloc.at[kind]).start()

    def to_whole_wait(kind, dst):
        part = dst.at[:, pl.ds(0, (wide - 1) * rows)]
        pltpu.make_async_copy(part, part, wr.at[kind]).wait()
        own = dst.at[:, pl.ds(0, rows)]
        pltpu.make_async_copy(own, own, wloc.at[kind]).wait()

    def from_whole(kind, src, dst):
        def send(d, carry):
            p = peer_of(d)
            pltpu.make_async_remote_copy(
                src_ref=mine_of(src, p, rows), dst_ref=dst.at[pl.ds(me * q, q)],
                send_sem=ws.at[kind], recv_sem=wr.at[kind], device_id={"wide": p}, device_id_type=MESH).start()
            return carry
        lax.fori_loop(1, wide, send, 0)
        pltpu.make_async_copy(mine_of(src, me, rows), dst.at[pl.ds(me * q, q)], wloc.at[kind]).start()

    def from_whole_wait(kind, dst):
        part = dst.at[pl.ds(0, (wide - 1) * q)]
        pltpu.make_async_copy(part, part, wr.at[kind]).wait()
        own = dst.at[pl.ds(0, q)]
        pltpu.make_async_copy(own, own, wloc.at[kind]).wait()

    def wide_sent(kind, src):
        part = src.at[pl.ds(0, (wide - 1) * q)] if src.shape[0] == second else src.at[:, pl.ds(0, (wide - 1) * rows)]
        pltpu.make_async_copy(part, part, ws.at[kind]).wait()

    by_first = pl.BlockSpec((step, second, third), lambda i: (i, 0, 0))
    by_second = pl.BlockSpec((second, step, third), lambda i: (0, i, 0))
    one_row = pl.BlockSpec((1, second, third), lambda i: (i, 0, 0))
    one_whole = pl.BlockSpec((1, full, third), lambda i: (i, 0, 0))

    def swapped(src_ref, g):
        return jnp.swapaxes(src_ref[:, 8 * g:8 * g + 8, :], 0, 1)

    def transpose_stage(src, dst):
        def body(x, out):
            for g in range(second // 8):
                out[8 * g:8 * g + 8, :, :] = jnp.swapaxes(x[:, 8 * g:8 * g + 8, :], 0, 1)
        pltpu.emit_pipeline(body, grid=(nc,), in_specs=[by_first], out_specs=[by_second])(src, dst)

    def third_dot(x, mh, ml):
        xh, xl = halves(x)
        return dot3(xh, xl, mh[...], ml[...])

    group = 32

    def phi_stage(src, dst):
        def body(x, out):
            for g in range(second // group):
                block = x[group * g:group * (g + 1)].reshape(group * step, third)
                result = third_dot(block, c3h, c3l).reshape(group, step, third)
                out[:, group * g:group * (g + 1), :] = jnp.swapaxes(result, 0, 1)
        pltpu.emit_pipeline(body, grid=(nc,), in_specs=[by_second], out_specs=[by_first])(src, dst)

    def coupled_stage(src, dst):
        def body(x, out):
            for g in range(second // group):
                block = x[:, group * g:group * (g + 1), :].reshape(group * step, third)
                result = third_dot(block, c3h, c3l).reshape(step, group, third)
                out[group * g:group * (g + 1), :, :] = jnp.swapaxes(result, 0, 1)
        pltpu.emit_pipeline(body, grid=(nc,), in_specs=[by_first], out_specs=[by_second])(src, dst)

    def base_stage(field, returned, dst, extra=None):
        def body(x, v, back, *rest):
            out = rest[-1]
            for g in range(second // group):
                cut = slice(group * g, group * (g + 1))
                block = x[:, cut, :].reshape(group * step, third)
                result = third_dot(block, k3h, k3l).reshape(step, group, third)
                result = result + v[:, cut, :] * x[:, cut, :] + jnp.swapaxes(back[cut], 0, 1)
                if extra is not None:
                    result = result + rest[0][:, cut, :]
                out[:, cut, :] = result
        ins = [field, pot, returned] + ([] if extra is None else [extra])
        specs = [by_first, by_first, by_second] + ([] if extra is None else [by_first])
        pltpu.emit_pipeline(body, grid=(nc,), in_specs=specs, out_specs=[by_first])(*ins, dst)

    def first_stage(terms, dst):
        def body(*args):
            out = args[-1]
            total = None
            for (_, mh, ml), x in zip(terms, args[:-1]):
                xh, xl = halves(x[0])
                value = dot3(mh[...], ml[...], xh, xl)
                total = value if total is None else total + value
            out[0] = total
        pltpu.emit_pipeline(body, grid=(q,), in_specs=[one_whole] * len(terms), out_specs=[one_whole])(
            *[t[0] for t in terms], dst)

    def place(slot, x):
        at = pl.ds(pl.multiple_of(slot * second, second), second)
        high, low = halves(x)
        fh[at, :] = high
        fl[at, :] = low

    def gather_stage(c):
        def body(own, e, o, f, y, v, ye, ve):
            place(z, own[0])
            place(end, e[0])
            place(other, o[0])
            place(far, f[0])
            for n, out in enumerate((y, ye, v, ve)):
                cut = slice(n * second, (n + 1) * second)
                out[0] = dot3(wh[cut, :], wl[cut, :], fh[...], fl[...])
        pltpu.emit_pipeline(body, grid=(step,), in_specs=[one_row] * 4, out_specs=[one_row] * 4)(
            piece(s0, c), piece(buf["end0"], c), piece(buf["other0"], c), piece(buf["far0"], c),
            piece(buf["y0"], c), piece(buf["w0"], c), piece(buf["sy"], c), piece(buf["sw"], c))

    def scatter_stage(c):
        def body(own, e, pown, pend, yo, ye, ao, af):
            place(0, own[0])
            place(1, e[0])
            place(2, pown[0])
            place(3, pend[0])
            for n in range(4):
                cut = slice(n * second, (n + 1) * second)
                gather[n] = dot3(wth[cut, :], wtl[cut, :], fh[...], fl[...])
            yo[0] = gather[z]
            ye[0] = gather[end]
            ao[0] = gather[other]
            af[0] = gather[far]
        pltpu.emit_pipeline(body, grid=(step,), in_specs=[one_row] * 4, out_specs=[one_row] * 4)(
            piece(s1, c), piece(buf["psie"], c), piece(buf["phi"], c), piece(buf["phie"], c),
            piece(buf["po"], c), piece(buf["pe"], c), piece(buf["ao"], c), piece(buf["af"], c))

    def finish_stage(c):
        def body(po, pe, a0, a1, y, ye):
            y[...] = po[...] + a0[...]
            ye[...] = pe[...] + a1[...]
        two = pl.BlockSpec((2, second, third), lambda i: (i, 0, 0))
        pltpu.emit_pipeline(body, grid=(step // 2,), in_specs=[two] * 4, out_specs=[two] * 2)(
            piece(buf["po"], c), piece(buf["pe"], c), piece(buf["ba0"], c), piece(buf["ba1"], c),
            piece(buf["y1"], c), piece(buf["se"], c))

    @pl.when(hub)
    def _():
        for c in range(min(2, nc)):
            zcopy(OWN, c, s0, buf["other0"], other).start()

    @pl.when(jnp.logical_not(hub))
    def _():
        each_chunk(lambda c: zcopy(END, c, s0, buf["end0"], my_hub).start())

    transpose_stage(s1, buf["s1b"])
    to_whole(TO_S1, buf["s1b"], buf["t1"])
    for matrix, high, low in ((c1, c1h, c1l), (c3, c3h, c3l), (w, wh, wl), (wt, wth, wtl), (k1, k1h, k1l), (k3, k3h, k3l)):
        high[...], low[...] = halves(matrix[...])

    first_at = min(3, nc - 1)
    phi_at = min(5, nc - 1)
    base_at = nc
    coupled_at = nc + 1
    second_at = min(nc + 4, 2 * nc)
    last_at = max(2 * nc - 1, second_at)
    early = nc // 2

    def body(t, carry):
        @pl.when(jnp.logical_and(hub, t + 2 < nc))
        def _():
            zcopy(OWN, t + 2, s0, buf["other0"], other).start()

        @pl.when(jnp.logical_and(hub, t < nc))
        def _():
            zrecv(END, t, buf["end0"])
            zcopy(FWD, t, buf["end0"], buf["far0"], other).start()

        @pl.when(t == first_at)
        def _():
            to_whole_wait(TO_S1, buf["t1"])
            first_stage([(buf["t1"], c1h, c1l)], buf["rc"])
            from_whole(BACK_C, buf["rc"], buf["bc"])

            @pl.when(jnp.logical_not(hub))
            def _():
                for c in range(early):
                    zcopy(PSI, c, s1, buf["psie"], my_hub).start()
            first_stage([(buf["t1"], k1h, k1l)], buf["rk"])
            transpose_stage(s0, buf["s0b"])

        @pl.when(t == phi_at)
        def _():
            from_whole_wait(BACK_C, buf["bc"])
            phi_stage(buf["bc"], buf["phi"])

            @pl.when(jnp.logical_not(hub))
            def _():
                for c in range(nc):
                    if c >= early:
                        zcopy(PSI, c, s1, buf["psie"], my_hub).start()
                    zcopy(PHI, c, buf["phi"], buf["phie"], my_hub).start()
            from_whole(BACK_K, buf["rk"], buf["bk"])
            to_whole(TO_S0, buf["s0b"], buf["t0"])

        @pl.when(jnp.logical_and(hub, jnp.logical_and(t >= nc - 1, t <= 2 * nc - 2)))
        def _():
            c = t - (nc - 1)
            zrecv(PSI, c, buf["psie"])
            zrecv(PHI, c, buf["phie"])
            scatter_stage(c)
            zcopy(SUM_O, c, buf["ao"], buf["ba0"], other).start()
            zcopy(SUM_F, c, buf["af"], buf["ba1"], other).start()

        @pl.when(jnp.logical_and(hub, jnp.logical_and(t >= 1, t <= nc)))
        def _():
            c = t - 1
            zrecv(OWN, c, buf["other0"])
            zrecv(FWD, c, buf["far0"])
            gather_stage(c)
            zcopy(WROW, c, buf["sw"], buf["w0"], end).start()
            zcopy(YROW, c, buf["sy"], buf["y0"], end).start()

        @pl.when(jnp.logical_and(hub, t >= nc + 1))
        def _():
            c = t - (nc + 1)
            zrecv(SUM_O, c, buf["ba0"])
            zrecv(SUM_F, c, buf["ba1"])
            finish_stage(c)
            zcopy(YEND, c, buf["se"], buf["y1"], end).start()

        @pl.when(t == base_at)
        def _():
            from_whole_wait(BACK_K, buf["bk"])
            base_stage(s1, buf["bk"], buf["base1"])

        @pl.when(t == coupled_at)
        def _():
            @pl.when(jnp.logical_not(hub))
            def _():
                each_chunk(lambda c: zrecv(WROW, c, buf["w0"]))
            coupled_stage(buf["w0"], buf["w0b"])
            to_whole(TO_W0, buf["w0b"], buf["tw"])

        @pl.when(t == second_at)
        def _():
            to_whole_wait(TO_S0, buf["t0"])
            to_whole_wait(TO_W0, buf["tw"])
            first_stage([(buf["t0"], k1h, k1l), (buf["tw"], c1h, c1l)], buf["r0"])
            from_whole(BACK_0, buf["r0"], buf["b0"])

        @pl.when(t == last_at)
        def _():
            @pl.when(jnp.logical_not(hub))
            def _():
                each_chunk(lambda c: zrecv(YROW, c, buf["y0"]))
            from_whole_wait(BACK_0, buf["b0"])
            base_stage(s0, buf["b0"], buf["h0"], buf["y0"])
        return carry

    lax.fori_loop(0, 2 * nc + 1, body, 0)

    @pl.when(hub)
    def _():
        def sent(c):
            for kind, name in ((OWN, "s"), (FWD, "end0"), (YROW, "sy"), (WROW, "sw"), (SUM_O, "ao"), (SUM_F, "af"), (YEND, "se")):
                zsent(kind, c, s0 if name == "s" else buf[name])
        each_chunk(sent)

    @pl.when(jnp.logical_not(hub))
    def _():
        def sent(c):
            zsent(END, c, s0)
            zsent(PSI, c, s1)
            zsent(PHI, c, buf["phi"])
            zrecv(YEND, c, buf["y1"])
        each_chunk(sent)

    for kind, name in ((TO_S1, "s1b"), (BACK_C, "rc"), (BACK_K, "rk"), (TO_S0, "s0b"), (TO_W0, "w0b"), (BACK_0, "r0")):
        wide_sent(kind, buf[name])


def section_kernel(wave, slope, out):
    out[...] = wave[...] + half_step * slope[...]


def result_kernel(wave, h0, y1, base1, slope, following):
    first = y1[...] + base1[...]
    second = -h0[...]
    slope[0] = first
    slope[1] = second
    following[0] = wave[0] + half_step * first
    following[1] = wave[1] + half_step * second


def local(wide, wavefunction, previous_slope, potential, kinetic_one, coupling_one, kinetic_two, coupling_two, kinetic_three, coupling_three):
    _, rows, second, third = wavefunction.shape
    full = rows * wide
    q = second // wide
    own = jnp.stack([kinetic_two, coupling_two])
    ends = lax.ppermute(own, "narrow", [(0, 1), (3, 2)])
    w = jnp.concatenate([own[0], ends[0], own[1], ends[1]], axis=0)
    wt = w.T

    block = 8
    pair = pl.BlockSpec((2, block, second, third), lambda i: (0, i, 0, 0))
    section = pl.pallas_call(
        section_kernel, grid=(rows // block,), in_specs=[pair, pair], out_specs=pair,
        out_shape=jax.ShapeDtypeStruct(wavefunction.shape, jnp.float32),
        compiler_params=pltpu.CompilerParams(vmem_limit_bytes=40 * 2**20),
        cost_estimate=pl.CostEstimate(flops=wavefunction.size * 2, bytes_accessed=wavefunction.size * 12, transcendentals=0),
    )(wavefunction, previous_slope)

    shapes = []
    for name in BUFFERS:
        if name in WIDE_SHAPED:
            shape = (q, full, third)
        elif name in SECOND_FIRST:
            shape = (second, rows, third)
        else:
            shape = (rows, second, third)
        shapes.append(jax.ShapeDtypeStruct(shape, jnp.float32))
    nc = rows // 8
    bf = jnp.bfloat16
    everything = 4 * second
    outs = pl.pallas_call(
        functools.partial(kernel, wide),
        out_shape=shapes,
        in_specs=[pl.BlockSpec(memory_space=pl.ANY)] * 2 + [pl.BlockSpec(memory_space=pltpu.VMEM)] * 6,
        out_specs=[pl.BlockSpec(memory_space=pl.ANY)] * len(BUFFERS),
        scratch_shapes=[pltpu.VMEM((everything, everything), bf)] * 4
        + [pltpu.VMEM((full, full), bf)] * 4
        + [pltpu.VMEM((third, third), bf)] * 4
        + [
            pltpu.VMEM((everything, third), bf),
            pltpu.VMEM((everything, third), bf),
            pltpu.VMEM((4, second, third), jnp.float32),
            pltpu.SemaphoreType.DMA((10, nc)),
            pltpu.SemaphoreType.DMA((10, nc)),
            pltpu.SemaphoreType.DMA((6,)),
            pltpu.SemaphoreType.DMA((6,)),
            pltpu.SemaphoreType.DMA((6,)),
        ],
        compiler_params=pltpu.CompilerParams(collective_id=0, has_side_effects=True, vmem_limit_bytes=52 * 2**20),
        cost_estimate=pl.CostEstimate(flops=6 * 3584 * 2 * rows * second * third * 2, bytes_accessed=40 * rows * second * third * 4, transcendentals=0),
    )(section, potential, w, wt, kinetic_one, coupling_one, kinetic_three, coupling_three)
    buf = dict(zip(BUFFERS, outs))

    one = pl.BlockSpec((block, second, third), lambda i: (i, 0, 0))
    return pl.pallas_call(
        result_kernel, grid=(rows // block,), in_specs=[pair, one, one, one], out_specs=[pair, pair],
        out_shape=[jax.ShapeDtypeStruct(wavefunction.shape, jnp.float32)] * 2,
        compiler_params=pltpu.CompilerParams(vmem_limit_bytes=40 * 2**20),
        cost_estimate=pl.CostEstimate(flops=wavefunction.size * 3, bytes_accessed=wavefunction.size * 18, transcendentals=0),
    )(wavefunction, buf["h0"], buf["y1"], buf["base1"])


def solution(mesh):
    wide = mesh.shape["wide"]
    field = P(None, "wide", "narrow", None)
    in_specs = (field, field, P("wide", "narrow", None), P(), P(), P("narrow", None), P("narrow", None), P(), P())

    def body(*arrays):
        return tuple(local(wide, *arrays))

    def run(*arrays):
        with jax.sharding.use_abstract_mesh(mesh.abstract_mesh):
            return jax.shard_map(body, mesh=mesh, in_specs=in_specs, out_specs=(field, field), check_vma=False)(*arrays)

    return run
```

time: 1560 us -> 813 us (0.52)
  waiting for transfers between devices: 836 us -> 0.01 us
  Pallas kernels: 0 us -> 794 us
  matrix products: 315 us -> 0 us
  local copies, waits for them, and re-layouts: 203 us -> 5.9 us
  starting transfers between devices: 110 us -> 4.19 us
  other arithmetic: 77.8 us -> 1.14 us
    pallas_call x0 -> x3, Pallas kernels: none -> 794 us  [the longest x1 754 us: local(): pl.pallas_call(functools.partial(kernel, wide), out_shape=shapes, in_spec...]
    ppermute x22 -> x1, waiting for transfers between devices: 774 us -> 0.01 us  [local(): ends = lax.ppermute(own, 'narrow', [(0, 1), (3, 2)])]
    dot_general x26 -> x0, matrix products: 315 us -> none  [the longest x16 176 us: along_two(): return jnp.einsum('ij,kjl->kil', matrix, field, precision=HIGH)]
    unnamed x38 -> x8, local copies, waits for them, and re-layouts: 81.7 us -> 5.53 us
    all_to_all x6 -> x0, waiting for transfers between devices: 62.3 us -> none  [the longest x4 42.1 us: to_whole_one(): lax.all_to_all(blocks, 'wide', split_axis=0, concat_axis=0, tiled=True)]
    ppermute x22 -> x1, starting transfers between devices: 60.8 us -> 4.19 us  [local(): ends = lax.ppermute(own, 'narrow', [(0, 1), (3, 2)])]
    add x6 -> x0, other arithmetic: 54.5 us -> none  [the longest x1 21.1 us: local(): next_input = wavefunction + half_step * slope]
    all_to_all x6 -> x0, starting transfers between devices: 49.4 us -> none  [the longest x4 31.8 us: to_whole_one(): lax.all_to_all(blocks, 'wide', split_axis=0, concat_axis=0, tiled=True)]
  transfers between devices with their start and end apart: 28 -> 1, of which waited for: 14 -> 0; matrix products, arithmetic and copies ran while one was open for 26% -> 0% of each run, Pallas kernels for 0% -> 2%
where the time goes in v1:
time: 813 us; the launch traced here: 806 us
  Pallas kernels  794 us (98%)
    pallas_call x1, Pallas kernels, local(): pl.pallas_call(functools.partial(kernel, wide), out_shape=shapes, in_spec...  754 us
    pallas_call x1, Pallas kernels, local(): pl.pallas_call(result_kernel, grid=(rows // block,), in_specs=[pair, one,...  23 us
    pallas_call x1, Pallas kernels, local(): pl.pallas_call(section_kernel, grid=(rows // block,), in_specs=[pair, pai...  17.3 us
  transfers between devices with their start and end apart: 1, of which 0 were waited for; matrix products, arithmetic and copies ran while one was open for 0% of the time, Pallas kernels for 2%

profile of v1, /device:TPU:1, one launch (start us, length us, event | category | flops | bytes accessed | tf_op | source)
XLA Modules:
  0.0 805.9 jit_solution(6704085171210166475)
XLA Ops:
  0.6 1.1 copy.13
  1.7 1.1 copy.12
  2.8 0.0 copy-start.1
  2.8 0.0 copy-start.2
  2.9 4.2 collective-permute-start
  7.1 17.3 %shard_map.104.s = f32[2,64,128,256]{3,2,1,0:T(8,128)} custom-call(f32[2,64,128,256]{3,2,1,0:T(8,128)} %wave.3, f32[2,64,128,256]{3,2,1,0:T(8,128)} %slope.1), custom_call_target="tpu_custom_call" | custom-call | flops 8388608 | bytes 50331648 | tf_op jit(solution)/shard_map/pallas_call | solution.py:401
  24.4 0.0 collective-permute-done
  24.4 1.1 fusion
  25.6 0.3 copy.15.w
  25.9 0.0 copy-done.1
  25.9 0.0 copy-done.2
  25.9 753.6 %shard_map.105 = (f32[64,128,256]{2,1,0:T(8,128)}, f32[64,128,256]{2,1,0:T(8,128)}, f32[64,128,256]{2,1,0:T(8,128)}, f32[64,128,256]{2,1,0:T(8,128)}, f32[64,128...) custom-call(f32[2,64,128,256]{3,2,1,0:T(8,128)} %shard_map.104.s, ...), custom_call_target="tpu_custom_call" | custom-call | flops 180388626432 | bytes 335544320 | tf_op jit(solution)/shard_map/pallas_call | solution.py:420
  779.6 0.0 copy-start
  779.6 3.4 copy-done
  782.9 23.0 %shard_map.106 = (f32[2,64,128,256]{3,2,1,0:T(8,128)}, f32[2,64,128,256]{3,2,1,0:T(8,128)}) custom-call(f32[2,64,128,256]{3,2,1,0:T(8,128)} %wave.3, f32[64,128,256]{2,1,0:T(8,128)S(1)} %copy-done, f32[64,128,256]{2,1,0:T(8,128)} %get-tuple-element.6.y1, f32[64,128,256]{2,1,0:T(8,128)} %get-tuple-element.7.base1), custom_call_target="tpu_custom_call" | custom-call | flops 12582912 | bytes 75497472 | tf_op jit(solution)/shard_map/pallas_call | solution.py:444
  (2 shorter events, 0.1 us)
Async XLA Ops:
  2.8 23.1 %copy-start.1 = (f32[256,256]{1,0:T(8,128)S(1)}, f32[256,256]{1,0:T(8,128)}, u32[]{:S(2)}) copy-start(f32[256,256]{1,0:T(8,128)} %k3.1) | copy-start | bytes 786436
  2.8 23.1 %copy-start.2 = (f32[256,256]{1,0:T(8,128)S(1)}, f32[256,256]{1,0:T(8,128)}, u32[]{:S(2)}) copy-start(f32[256,256]{1,0:T(8,128)} %c3.1) | copy-start | bytes 786436
  2.9 21.5 %collective-permute-start = (f32[2,128,512]{1,2,0:T(8,128)S(1)}, f32[2,128,512]{1,2,0:T(8,128)S(1)}, u32[]{:S(2)}, u32[]{:S(2)}) collective-permute-start(f32[2,128,512]{1,2,0:T(8,128)S(1)} %pad_maximum_fusion.1), channel_id=1, source_target_pairs={{0,1},{3,2},{4,5},{7,6},{8,9},{11,10},{12,13},{15,14},{16,17},{19,... | collective-permute-start | bytes 1572872 | tf_op jit(solution)/shard_map/ppermute | solution.py:395
  779.6 3.4 copy-start

commit v2 on v1

--- a/solution.py
+++ b/solution.py
@@ -15,7 +15,7 @@
     "end0", "other0", "far0", "y0", "w0", "sy", "sw",
     "s0b", "t0", "w0b", "tw", "r0", "b0",
     "s1b", "t1", "rc", "rk", "bc", "bk", "phi",
-    "psie", "phie", "po", "pe", "ao", "af", "ba0", "ba1", "se", "y1", "base1", "h0",
+    "psie", "phie", "po", "pe", "ao", "af", "ba0", "ba1", "se", "y1", "s0", "s1",
 )
 WIDE_SHAPED = ("t0", "tw", "r0", "t1", "rc", "rk")
 SECOND_FIRST = ("s0b", "w0b", "b0", "s1b", "bc", "bk")
@@ -31,11 +31,11 @@
     return dot(ah, bh) + dot(ah, bl) + dot(al, bh)
 
 
-def kernel(wide, s, pot, w, wt, k1, c1, k3, c3, *refs):
+def kernel(wide, wave, prev, pot, k2, c2, k1, c1, k3, c3, *refs):
     buf = dict(zip(BUFFERS, refs[:len(BUFFERS)]))
-    (wh, wl, wth, wtl, k1h, k1l, c1h, c1l, k3h, k3l, c3h, c3l, fh, fl, gather,
-     zs, zr, ws, wr, wloc) = refs[len(BUFFERS):]
-    rows, second, third = s.shape[1:]
+    (results, wh, wl, wth, wtl, k1h, k1l, c1h, c1l, k3h, k3l, c3h, c3l, fh, fl, gather, wend,
+     zs, zr, es, er, ws, wr, wloc) = refs[len(BUFFERS):]
+    rows, second, third = wave.shape[1:]
     full = rows * wide
     q = second // wide
     step = 8
@@ -47,7 +47,8 @@
     other = 3 - z
     far = 3 - end
     my_hub = jnp.where(z == 0, 1, 2)
-    s0, s1 = s.at[0], s.at[1]
+    slope, following = results.at[pl.ds(0, 2)], results.at[pl.ds(2, 2)]
+    s0, s1 = buf["s0"], buf["s1"]
 
     def peer_of(d):
         return lax.rem(me + d, wide)
@@ -64,12 +65,10 @@
     def _():
         pl.semaphore_signal(barrier, inc=1, device_id={"narrow": end}, device_id_type=MESH)
         pl.semaphore_signal(barrier, inc=1, device_id={"narrow": other}, device_id_type=MESH)
-        pl.semaphore_wait(barrier, wide + 1)
 
     @pl.when(jnp.logical_not(hub))
     def _():
         pl.semaphore_signal(barrier, inc=1, device_id={"narrow": my_hub}, device_id_type=MESH)
-        pl.semaphore_wait(barrier, wide)
 
     def piece(ref, c):
         return ref.at[pl.ds(pl.multiple_of(c * step, step), step)]
@@ -84,6 +83,11 @@
 
     def zsent(kind, c, src):
         pltpu.make_async_copy(piece(src, c), piece(src, c), zs.at[kind, c]).wait()
+
+    def end_matrix(n, matrix):
+        return pltpu.make_async_remote_copy(
+            src_ref=matrix, dst_ref=wend.at[n], send_sem=es.at[n], recv_sem=er.at[n],
+            device_id={"narrow": my_hub}, device_id_type=MESH)
 
     def each_chunk(f):
         def body(c, carry):
@@ -135,14 +139,33 @@
     one_row = pl.BlockSpec((1, second, third), lambda i: (i, 0, 0))
     one_whole = pl.BlockSpec((1, full, third), lambda i: (i, 0, 0))
 
-    def swapped(src_ref, g):
-        return jnp.swapaxes(src_ref[:, 8 * g:8 * g + 8, :], 0, 1)
+    parts = 2
+    half_first = pl.BlockSpec((step, second // parts, third), lambda i, j: (i, j, 0))
+    half_second = pl.BlockSpec((second // parts, step, third), lambda i, j: (j, i, 0))
+    quarter = pl.BlockSpec((step // 2, second, third), lambda i: (i, 0, 0))
 
     def transpose_stage(src, dst):
         def body(x, out):
             for g in range(second // 8):
                 out[8 * g:8 * g + 8, :, :] = jnp.swapaxes(x[:, 8 * g:8 * g + 8, :], 0, 1)
         pltpu.emit_pipeline(body, grid=(nc,), in_specs=[by_first], out_specs=[by_second])(src, dst)
+
+    def section_stage(start, size):
+        def body(x, y, out):
+            out[...] = x[...] + half_step * y[...]
+        cut = pl.ds(start, size)
+        pltpu.emit_pipeline(body, grid=(size * 2 // step,), in_specs=[quarter] * 2, out_specs=[quarter])(
+            wave.at[0, cut], prev.at[0, cut], s0.at[cut])
+
+    def section_swapped_stage():
+        def body(x, y, out, out_swapped):
+            for g in range(second // 8):
+                cut = slice(8 * g, 8 * g + 8)
+                value = x[:, cut, :] + half_step * y[:, cut, :]
+                out[:, cut, :] = value
+                out_swapped[cut, :, :] = jnp.swapaxes(value, 0, 1)
+        pltpu.emit_pipeline(body, grid=(nc,), in_specs=[by_first] * 2, out_specs=[by_first, by_second])(
+            wave.at[1], prev.at[1], s1, buf["s1b"])
 
     def third_dot(x, mh, ml):
         xh, xl = halves(x)
@@ -166,20 +189,23 @@
                 out[group * g:group * (g + 1), :, :] = jnp.swapaxes(result, 0, 1)
         pltpu.emit_pipeline(body, grid=(nc,), in_specs=[by_first], out_specs=[by_second])(src, dst)
 
-    def base_stage(field, returned, dst, extra=None):
-        def body(x, v, back, *rest):
-            out = rest[-1]
-            for g in range(second // group):
+    def base_stage(field, returned, start, sign, slot, extra=None):
+        def body(x, v, back, base, *rest):
+            out, out_next = rest[-2:]
+            for g in range(second // parts // group):
                 cut = slice(group * g, group * (g + 1))
                 block = x[:, cut, :].reshape(group * step, third)
                 result = third_dot(block, k3h, k3l).reshape(step, group, third)
                 result = result + v[:, cut, :] * x[:, cut, :] + jnp.swapaxes(back[cut], 0, 1)
                 if extra is not None:
                     result = result + rest[0][:, cut, :]
+                result = sign * result
                 out[:, cut, :] = result
-        ins = [field, pot, returned] + ([] if extra is None else [extra])
-        specs = [by_first, by_first, by_second] + ([] if extra is None else [by_first])
-        pltpu.emit_pipeline(body, grid=(nc,), in_specs=specs, out_specs=[by_first])(*ins, dst)
+                out_next[:, cut, :] = base[:, cut, :] + half_step * result
+        ins = [field, pot, returned, start] + ([] if extra is None else [extra])
+        specs = [half_first, half_first, half_second, half_first] + ([] if extra is None else [half_first])
+        pltpu.emit_pipeline(body, grid=(nc, parts), in_specs=specs, out_specs=[half_first] * 2)(
+            *ins, slope.at[slot], following.at[slot])
 
     def first_stage(terms, dst):
         def body(*args):
@@ -229,28 +255,64 @@
             piece(s1, c), piece(buf["psie"], c), piece(buf["phi"], c), piece(buf["phie"], c),
             piece(buf["po"], c), piece(buf["pe"], c), piece(buf["ao"], c), piece(buf["af"], c))
 
-    def finish_stage(c):
-        def body(po, pe, a0, a1, y, ye):
-            y[...] = po[...] + a0[...]
-            ye[...] = pe[...] + a1[...]
-        two = pl.BlockSpec((2, second, third), lambda i: (i, 0, 0))
-        pltpu.emit_pipeline(body, grid=(step // 2,), in_specs=[two] * 4, out_specs=[two] * 2)(
-            piece(buf["po"], c), piece(buf["pe"], c), piece(buf["ba0"], c), piece(buf["ba1"], c),
-            piece(buf["y1"], c), piece(buf["se"], c))
+    def end_sum_stage(c):
+        def body(x, y, out):
+            out[...] = x[...] + y[...]
+        pltpu.emit_pipeline(body, grid=(2,), in_specs=[quarter] * 2, out_specs=[quarter])(
+            piece(buf["pe"], c), piece(buf["ba1"], c), piece(buf["se"], c))
+
+    def own_sum_stage(c, *terms):
+        def body(*args):
+            value = args[0][...]
+            for term in args[1:-2]:
+                value = value + term[...]
+            args[-2][...] += value
+            args[-1][...] += half_step * value
+        pltpu.emit_pipeline(body, grid=(2,), in_specs=[quarter] * len(terms), out_specs=[quarter] * 2)(
+            *[piece(buf[term], c) for term in terms], piece(slope.at[0], c), piece(following.at[0], c))
+
+    ahead = min(3, nc)
+    section_stage(0, step)
 
     @pl.when(hub)
     def _():
-        for c in range(min(2, nc)):
-            zcopy(OWN, c, s0, buf["other0"], other).start()
+        pl.semaphore_wait(barrier, wide + 1)
+        zcopy(OWN, 0, s0, buf["other0"], other).start()
 
     @pl.when(jnp.logical_not(hub))
     def _():
-        each_chunk(lambda c: zcopy(END, c, s0, buf["end0"], my_hub).start())
-
-    transpose_stage(s1, buf["s1b"])
+        pl.semaphore_wait(barrier, wide)
+        zcopy(END, 0, s0, buf["end0"], my_hub).start()
+        for n, matrix in enumerate((k2, c2)):
+            end_matrix(n, matrix).start()
+
+    if nc > 1:
+        section_stage(step, rows - step)
+
+        @pl.when(hub)
+        def _():
+            for c in range(1, ahead):
+                zcopy(OWN, c, s0, buf["other0"], other).start()
+
+        @pl.when(jnp.logical_not(hub))
+        def _():
+            for c in range(1, nc):
+                zcopy(END, c, s0, buf["end0"], my_hub).start()
+
+    section_swapped_stage()
     to_whole(TO_S1, buf["s1b"], buf["t1"])
-    for matrix, high, low in ((c1, c1h, c1l), (c3, c3h, c3l), (w, wh, wl), (wt, wth, wtl), (k1, k1h, k1l), (k3, k3h, k3l)):
+    for matrix, high, low in ((c1, c1h, c1l), (c3, c3h, c3l), (k1, k1h, k1l), (k3, k3h, k3l)):
         high[...], low[...] = halves(matrix[...])
+
+    @pl.when(hub)
+    def _():
+        for n, matrix in enumerate((k2, c2)):
+            end_matrix(n, matrix).wait_recv()
+            for m, rows_of in enumerate((matrix, wend.at[n])):
+                cut = slice((2 * n + m) * second, (2 * n + m + 1) * second)
+                value = rows_of[...]
+                wh[cut, :], wl[cut, :] = halves(value)
+                wth[:, cut], wtl[:, cut] = halves(value.T)
 
     first_at = min(3, nc - 1)
     phi_at = min(5, nc - 1)
@@ -261,9 +323,9 @@
     early = nc // 2
 
     def body(t, carry):
-        @pl.when(jnp.logical_and(hub, t + 2 < nc))
-        def _():
-            zcopy(OWN, t + 2, s0, buf["other0"], other).start()
+        @pl.when(jnp.logical_and(hub, t + ahead < nc))
+        def _():
+            zcopy(OWN, t + ahead, s0, buf["other0"], other).start()
 
         @pl.when(jnp.logical_and(hub, t < nc))
         def _():
@@ -303,8 +365,8 @@
             zrecv(PSI, c, buf["psie"])
             zrecv(PHI, c, buf["phie"])
             scatter_stage(c)
+            zcopy(SUM_F, c, buf["af"], buf["ba1"], other).start()
             zcopy(SUM_O, c, buf["ao"], buf["ba0"], other).start()
-            zcopy(SUM_F, c, buf["af"], buf["ba1"], other).start()
 
         @pl.when(jnp.logical_and(hub, jnp.logical_and(t >= 1, t <= nc)))
         def _():
@@ -318,15 +380,16 @@
         @pl.when(jnp.logical_and(hub, t >= nc + 1))
         def _():
             c = t - (nc + 1)
+            zrecv(SUM_F, c, buf["ba1"])
+            end_sum_stage(c)
+            zcopy(YEND, c, buf["se"], buf["y1"], end).start()
             zrecv(SUM_O, c, buf["ba0"])
-            zrecv(SUM_F, c, buf["ba1"])
-            finish_stage(c)
-            zcopy(YEND, c, buf["se"], buf["y1"], end).start()
+            own_sum_stage(c, "po", "ba0")
 
         @pl.when(t == base_at)
         def _():
             from_whole_wait(BACK_K, buf["bk"])
-            base_stage(s1, buf["bk"], buf["base1"])
+            base_stage(s1, buf["bk"], wave.at[0], 1.0, 0)
 
         @pl.when(t == coupled_at)
         def _():
@@ -349,7 +412,7 @@
             def _():
                 each_chunk(lambda c: zrecv(YROW, c, buf["y0"]))
             from_whole_wait(BACK_0, buf["b0"])
-            base_stage(s0, buf["b0"], buf["h0"], buf["y0"])
+            base_stage(s0, buf["b0"], wave.at[1], -1.0, 1, buf["y0"])
         return carry
 
     lax.fori_loop(0, 2 * nc + 1, body, 0)
@@ -357,8 +420,8 @@
     @pl.when(hub)
     def _():
         def sent(c):
-            for kind, name in ((OWN, "s"), (FWD, "end0"), (YROW, "sy"), (WROW, "sw"), (SUM_O, "ao"), (SUM_F, "af"), (YEND, "se")):
-                zsent(kind, c, s0 if name == "s" else buf[name])
+            for kind, name in ((OWN, "s0"), (FWD, "end0"), (YROW, "sy"), (WROW, "sw"), (SUM_O, "ao"), (SUM_F, "af"), (YEND, "se")):
+                zsent(kind, c, buf[name])
         each_chunk(sent)
 
     @pl.when(jnp.logical_not(hub))
@@ -368,43 +431,30 @@
             zsent(PSI, c, s1)
             zsent(PHI, c, buf["phi"])
             zrecv(YEND, c, buf["y1"])
+            own_sum_stage(c, "y1")
         each_chunk(sent)
+        for n, matrix in enumerate((k2, c2)):
+            end_matrix(n, matrix).wait_send()
 
     for kind, name in ((TO_S1, "s1b"), (BACK_C, "rc"), (BACK_K, "rk"), (TO_S0, "s0b"), (TO_W0, "w0b"), (BACK_0, "r0")):
         wide_sent(kind, buf[name])
 
 
-def section_kernel(wave, slope, out):
-    out[...] = wave[...] + half_step * slope[...]
-
-
-def result_kernel(wave, h0, y1, base1, slope, following):
-    first = y1[...] + base1[...]
-    second = -h0[...]
-    slope[0] = first
-    slope[1] = second
-    following[0] = wave[0] + half_step * first
-    following[1] = wave[1] + half_step * second
+def write_kernel(results, slope_out, following_out, sems):
+    copies = [
+        pltpu.make_async_copy(results.at[pl.ds(0, 2)], slope_out, sems.at[0]),
+        pltpu.make_async_copy(results.at[pl.ds(2, 2)], following_out, sems.at[1]),
+    ]
+    for copy in copies:
+        copy.start()
+    for copy in copies:
+        copy.wait()
 
 
 def local(wide, wavefunction, previous_slope, potential, kinetic_one, coupling_one, kinetic_two, coupling_two, kinetic_three, coupling_three):
     _, rows, second, third = wavefunction.shape
     full = rows * wide
     q = second // wide
-    own = jnp.stack([kinetic_two, coupling_two])
-    ends = lax.ppermute(own, "narrow", [(0, 1), (3, 2)])
-    w = jnp.concatenate([own[0], ends[0], own[1], ends[1]], axis=0)
-    wt = w.T
-
-    block = 8
-    pair = pl.BlockSpec((2, block, second, third), lambda i: (0, i, 0, 0))
-    section = pl.pallas_call(
-        section_kernel, grid=(rows // block,), in_specs=[pair, pair], out_specs=pair,
-        out_shape=jax.ShapeDtypeStruct(wavefunction.shape, jnp.float32),
-        compiler_params=pltpu.CompilerParams(vmem_limit_bytes=40 * 2**20),
-        cost_estimate=pl.CostEstimate(flops=wavefunction.size * 2, bytes_accessed=wavefunction.size * 12, transcendentals=0),
-    )(wavefunction, previous_slope)
-
     shapes = []
     for name in BUFFERS:
         if name in WIDE_SHAPED:
@@ -414,14 +464,15 @@
         else:
             shape = (rows, second, third)
         shapes.append(jax.ShapeDtypeStruct(shape, jnp.float32))
+    shapes += [pltpu.VMEM((4, rows, second, third), jnp.float32)]
     nc = rows // 8
     bf = jnp.bfloat16
     everything = 4 * second
     outs = pl.pallas_call(
         functools.partial(kernel, wide),
         out_shape=shapes,
-        in_specs=[pl.BlockSpec(memory_space=pl.ANY)] * 2 + [pl.BlockSpec(memory_space=pltpu.VMEM)] * 6,
-        out_specs=[pl.BlockSpec(memory_space=pl.ANY)] * len(BUFFERS),
+        in_specs=[pl.BlockSpec(memory_space=pl.ANY)] * 3 + [pl.BlockSpec(memory_space=pltpu.VMEM)] * 6,
+        out_specs=[pl.BlockSpec(memory_space=pl.ANY)] * len(BUFFERS) + [pl.BlockSpec(memory_space=pltpu.VMEM)],
         scratch_shapes=[pltpu.VMEM((everything, everything), bf)] * 4
         + [pltpu.VMEM((full, full), bf)] * 4
         + [pltpu.VMEM((third, third), bf)] * 4
@@ -429,24 +480,27 @@
             pltpu.VMEM((everything, third), bf),
             pltpu.VMEM((everything, third), bf),
             pltpu.VMEM((4, second, third), jnp.float32),
+            pltpu.VMEM((2, second, everything), jnp.float32),
             pltpu.SemaphoreType.DMA((10, nc)),
             pltpu.SemaphoreType.DMA((10, nc)),
+            pltpu.SemaphoreType.DMA((2,)),
+            pltpu.SemaphoreType.DMA((2,)),
             pltpu.SemaphoreType.DMA((6,)),
             pltpu.SemaphoreType.DMA((6,)),
             pltpu.SemaphoreType.DMA((6,)),
         ],
-        compiler_params=pltpu.CompilerParams(collective_id=0, has_side_effects=True, vmem_limit_bytes=52 * 2**20),
+        compiler_params=pltpu.CompilerParams(collective_id=0, has_side_effects=True, vmem_limit_bytes=26 * 2**20),
         cost_estimate=pl.CostEstimate(flops=6 * 3584 * 2 * rows * second * third * 2, bytes_accessed=40 * rows * second * third * 4, transcendentals=0),
-    )(section, potential, w, wt, kinetic_one, coupling_one, kinetic_three, coupling_three)
-    buf = dict(zip(BUFFERS, outs))
-
-    one = pl.BlockSpec((block, second, third), lambda i: (i, 0, 0))
+    )(wavefunction, previous_slope, potential, kinetic_two, coupling_two, kinetic_one, coupling_one, kinetic_three, coupling_three)
     return pl.pallas_call(
-        result_kernel, grid=(rows // block,), in_specs=[pair, one, one, one], out_specs=[pair, pair],
+        write_kernel,
+        in_specs=[pl.BlockSpec(memory_space=pltpu.VMEM)],
+        out_specs=[pl.BlockSpec(memory_space=pl.ANY)] * 2,
         out_shape=[jax.ShapeDtypeStruct(wavefunction.shape, jnp.float32)] * 2,
-        compiler_params=pltpu.CompilerParams(vmem_limit_bytes=40 * 2**20),
-        cost_estimate=pl.CostEstimate(flops=wavefunction.size * 3, bytes_accessed=wavefunction.size * 18, transcendentals=0),
-    )(wavefunction, buf["h0"], buf["y1"], buf["base1"])
+        scratch_shapes=[pltpu.SemaphoreType.DMA((2,))],
+        compiler_params=pltpu.CompilerParams(vmem_limit_bytes=2**20),
+        cost_estimate=pl.CostEstimate(flops=0, bytes_accessed=wavefunction.size * 8, transcendentals=0),
+    )(*outs[len(BUFFERS):])
 
 
 def solution(mesh):

time: 813 us -> 754 us (0.927)
  Pallas kernels: 794 us -> 745 us
    pallas_call x2 -> x1, Pallas kernels: 40.3 us -> 11.7 us  [local(): pl.pallas_call(write_kernel, in_specs=[pl.BlockSpec(memory_space=pltpu.VM...]
    pallas_call x1, Pallas kernels: 754 us -> 734 us  [local(): pl.pallas_call(functools.partial(kernel, wide), out_shape=shapes, in_spec...]
  transfers between devices with their start and end apart: 1 -> 0, of which waited for: 0 -> 0; matrix products, arithmetic and copies ran while one was open for 0% -> 0% of each run, Pallas kernels for 2% -> 0%
where the time goes in v2:
time: 754 us; the launch traced here: 746 us
  Pallas kernels  745 us (99%)
    pallas_call x1, Pallas kernels, local(): pl.pallas_call(functools.partial(kernel, wide), out_shape=shapes, in_spec...  734 us

profile of v2, /device:TPU:1, one launch (start us, length us, event | category | flops | bytes accessed | tf_op | source)
XLA Modules:
  0.0 745.9 jit_solution(10649736120623691260)
XLA Ops:
  0.6 733.5 %shard_map.104 = (f32[64,128,256]{2,1,0:T(8,128)}, f32[64,128,256]{2,1,0:T(8,128)}, f32[64,128,256]{2,1,0:T(8,128)}, f32[64,128,256]{2,1,0:T(8,128)}, f32[64,128...) custom-call(f32[2,64,128,256]{3,2,1,0:T(8,128)} %wave.1, ...), custom_call_target="tpu_custom_call" | custom-call | flops 180388626432 | bytes 335544320 | tf_op jit(solution)/shard_map/pallas_call | solution.py:471
  734.2 11.7 %shard_map.105 = (f32[2,64,128,256]{3,2,1,0:T(8,128)}, f32[2,64,128,256]{3,2,1,0:T(8,128)}) custom-call(f32[4,64,128,256]{3,2,1,0:T(8,128)S(1)} %get-tuple-element.3.results), custom_call_target="tpu_custom_call" | custom-call | bytes 33554432 | tf_op jit(solution)/shard_map/pallas_call | solution.py:495

commit v3 on v2

--- a/solution.py
+++ b/solution.py
@@ -34,7 +34,7 @@
 def kernel(wide, wave, prev, pot, k2, c2, k1, c1, k3, c3, *refs):
     buf = dict(zip(BUFFERS, refs[:len(BUFFERS)]))
     (results, wh, wl, wth, wtl, k1h, k1l, c1h, c1l, k3h, k3l, c3h, c3l, fh, fl, gather, wend,
-     zs, zr, es, er, ws, wr, wloc) = refs[len(BUFFERS):]
+     k2v, c2v, k1v, c1v, k3v, c3v, zs, zr, es, er, ms, ws, wr, wloc) = refs[len(BUFFERS):]
     rows, second, third = wave.shape[1:]
     full = rows * wide
     q = second // wide
@@ -150,11 +150,13 @@
                 out[8 * g:8 * g + 8, :, :] = jnp.swapaxes(x[:, 8 * g:8 * g + 8, :], 0, 1)
         pltpu.emit_pipeline(body, grid=(nc,), in_specs=[by_first], out_specs=[by_second])(src, dst)
 
-    def section_stage(start, size):
+    def section_stage(start, size, block):
+        spec = pl.BlockSpec((block, second, third), lambda i: (i, 0, 0))
+
         def body(x, y, out):
             out[...] = x[...] + half_step * y[...]
         cut = pl.ds(start, size)
-        pltpu.emit_pipeline(body, grid=(size * 2 // step,), in_specs=[quarter] * 2, out_specs=[quarter])(
+        pltpu.emit_pipeline(body, grid=(size // block,), in_specs=[spec] * 2, out_specs=[spec])(
             wave.at[0, cut], prev.at[0, cut], s0.at[cut])
 
     def section_swapped_stage():
@@ -272,7 +274,7 @@
             *[piece(buf[term], c) for term in terms], piece(slope.at[0], c), piece(following.at[0], c))
 
     ahead = min(3, nc)
-    section_stage(0, step)
+    section_stage(0, step, step // 4)
 
     @pl.when(hub)
     def _():
@@ -286,8 +288,15 @@
         for n, matrix in enumerate((k2, c2)):
             end_matrix(n, matrix).start()
 
+    fetches = [
+        pltpu.make_async_copy(matrix, held, ms.at[n])
+        for n, (matrix, held) in enumerate(((k2, k2v), (c2, c2v), (k1, k1v), (c1, c1v), (k3, k3v), (c3, c3v)))
+    ]
+    for fetch in fetches:
+        fetch.start()
+
     if nc > 1:
-        section_stage(step, rows - step)
+        section_stage(step, rows - step, step // 2)
 
         @pl.when(hub)
         def _():
@@ -301,14 +310,16 @@
 
     section_swapped_stage()
     to_whole(TO_S1, buf["s1b"], buf["t1"])
-    for matrix, high, low in ((c1, c1h, c1l), (c3, c3h, c3l), (k1, k1h, k1l), (k3, k3h, k3l)):
+    for fetch in fetches:
+        fetch.wait()
+    for matrix, high, low in ((c1v, c1h, c1l), (c3v, c3h, c3l), (k1v, k1h, k1l), (k3v, k3h, k3l)):
         high[...], low[...] = halves(matrix[...])
 
     @pl.when(hub)
     def _():
-        for n, matrix in enumerate((k2, c2)):
+        for n, (matrix, held) in enumerate(((k2, k2v), (c2, c2v))):
             end_matrix(n, matrix).wait_recv()
-            for m, rows_of in enumerate((matrix, wend.at[n])):
+            for m, rows_of in enumerate((held, wend.at[n])):
                 cut = slice((2 * n + m) * second, (2 * n + m + 1) * second)
                 value = rows_of[...]
                 wh[cut, :], wl[cut, :] = halves(value)
@@ -319,7 +330,7 @@
     base_at = nc
     coupled_at = nc + 1
     second_at = min(nc + 4, 2 * nc)
-    last_at = max(2 * nc - 1, second_at)
+    last_at = max(2 * nc - 2, second_at)
     early = nc // 2
 
     def body(t, carry):
@@ -366,7 +377,14 @@
             zrecv(PHI, c, buf["phie"])
             scatter_stage(c)
             zcopy(SUM_F, c, buf["af"], buf["ba1"], other).start()
-            zcopy(SUM_O, c, buf["ao"], buf["ba0"], other).start()
+
+            @pl.when(jnp.logical_and(c == nc - 1, nc > 1))
+            def _():
+                zcopy(SUM_O, max(nc - 2, 0), buf["ao"], buf["ba0"], other).start()
+
+            @pl.when(c != nc - 2)
+            def _():
+                zcopy(SUM_O, c, buf["ao"], buf["ba0"], other).start()
 
         @pl.when(jnp.logical_and(hub, jnp.logical_and(t >= 1, t <= nc)))
         def _():
@@ -380,9 +398,14 @@
         @pl.when(jnp.logical_and(hub, t >= nc + 1))
         def _():
             c = t - (nc + 1)
-            zrecv(SUM_F, c, buf["ba1"])
-            end_sum_stage(c)
-            zcopy(YEND, c, buf["se"], buf["y1"], end).start()
+            here = jnp.where(c == nc - 2, 2, jnp.where(c == nc - 1, 1 if nc == 1 else 0, 1))
+
+            def far_sum(e, carry):
+                zrecv(SUM_F, e, buf["ba1"])
+                end_sum_stage(e)
+                zcopy(YEND, e, buf["se"], buf["y1"], end).start()
+                return carry
+            lax.fori_loop(c, c + here, far_sum, 0)
             zrecv(SUM_O, c, buf["ba0"])
             own_sum_stage(c, "po", "ba0")
 
@@ -471,7 +494,7 @@
     outs = pl.pallas_call(
         functools.partial(kernel, wide),
         out_shape=shapes,
-        in_specs=[pl.BlockSpec(memory_space=pl.ANY)] * 3 + [pl.BlockSpec(memory_space=pltpu.VMEM)] * 6,
+        in_specs=[pl.BlockSpec(memory_space=pl.ANY)] * 9,
         out_specs=[pl.BlockSpec(memory_space=pl.ANY)] * len(BUFFERS) + [pl.BlockSpec(memory_space=pltpu.VMEM)],
         scratch_shapes=[pltpu.VMEM((everything, everything), bf)] * 4
         + [pltpu.VMEM((full, full), bf)] * 4
@@ -481,10 +504,16 @@
             pltpu.VMEM((everything, third), bf),
             pltpu.VMEM((4, second, third), jnp.float32),
             pltpu.VMEM((2, second, everything), jnp.float32),
+        ]
+        + [pltpu.VMEM((second, everything), jnp.float32)] * 2
+        + [pltpu.VMEM((full, full), jnp.float32)] * 2
+        + [pltpu.VMEM((third, third), jnp.float32)] * 2
+        + [
             pltpu.SemaphoreType.DMA((10, nc)),
             pltpu.SemaphoreType.DMA((10, nc)),
             pltpu.SemaphoreType.DMA((2,)),
             pltpu.SemaphoreType.DMA((2,)),
+            pltpu.SemaphoreType.DMA((6,)),
             pltpu.SemaphoreType.DMA((6,)),
             pltpu.SemaphoreType.DMA((6,)),
             pltpu.SemaphoreType.DMA((6,)),

time: 754 us -> 747 us (level)
  Pallas kernels: 745 us -> 736 us
    pallas_call x1, Pallas kernels: 734 us -> 725 us  [local(): pl.pallas_call(functools.partial(kernel, wide), out_shape=shapes, in_spec...]
where the time goes in v3:
time: 747 us; the launch traced here: 737 us
  Pallas kernels  736 us (99%)
    pallas_call x1, Pallas kernels, local(): pl.pallas_call(functools.partial(kernel, wide), out_shape=shapes, in_spec...  725 us

profile of v3, /device:TPU:1, one launch (start us, length us, event | category | flops | bytes accessed | tf_op | source)
XLA Modules:
  0.0 737.0 jit_solution(10470167976576475701)
XLA Ops:
  0.6 724.7 %shard_map.104 = (f32[64,128,256]{2,1,0:T(8,128)}, f32[64,128,256]{2,1,0:T(8,128)}, f32[64,128,256]{2,1,0:T(8,128)}, f32[64,128,256]{2,1,0:T(8,128)}, f32[64,128...) custom-call(f32[2,64,128,256]{3,2,1,0:T(8,128)} %wave.1, ...), custom_call_target="tpu_custom_call" | custom-call | flops 180388626432 | bytes 335544320 | tf_op jit(solution)/shard_map/pallas_call | solution.py:494
  725.3 11.7 %shard_map.105 = (f32[2,64,128,256]{3,2,1,0:T(8,128)}, f32[2,64,128,256]{3,2,1,0:T(8,128)}) custom-call(f32[4,64,128,256]{3,2,1,0:T(8,128)S(1)} %get-tuple-element.3.results), custom_call_target="tpu_custom_call" | custom-call | bytes 33554432 | tf_op jit(solution)/shard_map/pallas_call | solution.py:524

commit v4 on v3

--- a/solution.py
+++ b/solution.py
@@ -33,7 +33,7 @@
 
 def kernel(wide, wave, prev, pot, k2, c2, k1, c1, k3, c3, *refs):
     buf = dict(zip(BUFFERS, refs[:len(BUFFERS)]))
-    (results, wh, wl, wth, wtl, k1h, k1l, c1h, c1l, k3h, k3l, c3h, c3l, fh, fl, gather, wend,
+    (results, wh, wl, wth, wtl, k1h, k1l, c1h, c1l, k3h, k3l, c3h, c3l, fh, fl, gather, wend, land,
      k2v, c2v, k1v, c1v, k3v, c3v, zs, zr, es, er, ms, ws, wr, wloc) = refs[len(BUFFERS):]
     rows, second, third = wave.shape[1:]
     full = rows * wide
@@ -88,6 +88,11 @@
         return pltpu.make_async_remote_copy(
             src_ref=matrix, dst_ref=wend.at[n], send_sem=es.at[n], recv_sem=er.at[n],
             device_id={"narrow": my_hub}, device_id_type=MESH)
+
+    def last_near():
+        return pltpu.make_async_remote_copy(
+            src_ref=buf["ao"].at[pl.ds(rows - step, step)], dst_ref=land, send_sem=zs.at[SUM_O, nc - 1],
+            recv_sem=zr.at[SUM_O, nc - 1], device_id={"narrow": other}, device_id_type=MESH)
 
     def each_chunk(f):
         def body(c, carry):
@@ -274,16 +279,36 @@
             *[piece(buf[term], c) for term in terms], piece(slope.at[0], c), piece(following.at[0], c))
 
     ahead = min(3, nc)
-    section_stage(0, step, step // 4)
+    small = step // 4
+
+    def first_piece(i):
+        at = pl.ds(i * small, small)
+        pltpu.make_async_remote_copy(
+            src_ref=s0.at[at], dst_ref=buf["other0"].at[at], send_sem=zs.at[OWN, 0], recv_sem=zr.at[OWN, 0],
+            device_id={"narrow": other}, device_id_type=MESH).start()
+
+    section_stage(0, small, small)
 
     @pl.when(hub)
     def _():
         pl.semaphore_wait(barrier, wide + 1)
-        zcopy(OWN, 0, s0, buf["other0"], other).start()
+        first_piece(0)
 
     @pl.when(jnp.logical_not(hub))
     def _():
         pl.semaphore_wait(barrier, wide)
+
+    def next_piece(i, carry):
+        section_stage(i * small, small, small)
+
+        @pl.when(hub)
+        def _():
+            first_piece(i)
+        return carry
+    lax.fori_loop(1, step // small, next_piece, 0)
+
+    @pl.when(jnp.logical_not(hub))
+    def _():
         zcopy(END, 0, s0, buf["end0"], my_hub).start()
         for n, matrix in enumerate((k2, c2)):
             end_matrix(n, matrix).start()
@@ -382,7 +407,11 @@
             def _():
                 zcopy(SUM_O, max(nc - 2, 0), buf["ao"], buf["ba0"], other).start()
 
-            @pl.when(c != nc - 2)
+            @pl.when(c == nc - 1)
+            def _():
+                last_near().start()
+
+            @pl.when(c < nc - 2)
             def _():
                 zcopy(SUM_O, c, buf["ao"], buf["ba0"], other).start()
 
@@ -406,8 +435,15 @@
                 zcopy(YEND, e, buf["se"], buf["y1"], end).start()
                 return carry
             lax.fori_loop(c, c + here, far_sum, 0)
-            zrecv(SUM_O, c, buf["ba0"])
-            own_sum_stage(c, "po", "ba0")
+
+            @pl.when(c < nc - 1)
+            def _():
+                zrecv(SUM_O, c, buf["ba0"])
+                own_sum_stage(c, "po", "ba0")
+
+            @pl.when(c == nc - 1)
+            def _():
+                own_sum_stage(c, "po")
 
         @pl.when(t == base_at)
         def _():
@@ -440,12 +476,25 @@
 
     lax.fori_loop(0, 2 * nc + 1, body, 0)
 
+    for kind, name in ((TO_S1, "s1b"), (BACK_C, "rc"), (BACK_K, "rk"), (TO_S0, "s0b"), (TO_W0, "w0b"), (BACK_0, "r0")):
+        wide_sent(kind, buf[name])
+
     @pl.when(hub)
     def _():
         def sent(c):
-            for kind, name in ((OWN, "s0"), (FWD, "end0"), (YROW, "sy"), (WROW, "sw"), (SUM_O, "ao"), (SUM_F, "af"), (YEND, "se")):
+            for kind, name in ((OWN, "s0"), (FWD, "end0"), (YROW, "sy"), (WROW, "sw"), (SUM_F, "af"), (YEND, "se")):
                 zsent(kind, c, buf[name])
+
+            @pl.when(c < nc - 1)
+            def _():
+                zsent(SUM_O, c, buf["ao"])
         each_chunk(sent)
+        last_near().wait_recv()
+        tail = slice(rows - step, rows)
+        value = land[...]
+        results[0, tail] = results[0, tail] + value
+        results[2, tail] = results[2, tail] + half_step * value
+        last_near().wait_send()
 
     @pl.when(jnp.logical_not(hub))
     def _():
@@ -458,9 +507,6 @@
         each_chunk(sent)
         for n, matrix in enumerate((k2, c2)):
             end_matrix(n, matrix).wait_send()
-
-    for kind, name in ((TO_S1, "s1b"), (BACK_C, "rc"), (BACK_K, "rk"), (TO_S0, "s0b"), (TO_W0, "w0b"), (BACK_0, "r0")):
-        wide_sent(kind, buf[name])
 
 
 def write_kernel(results, slope_out, following_out, sems):
@@ -504,6 +550,7 @@
             pltpu.VMEM((everything, third), bf),
             pltpu.VMEM((4, second, third), jnp.float32),
             pltpu.VMEM((2, second, everything), jnp.float32),
+            pltpu.VMEM((8, second, third), jnp.float32),
         ]
         + [pltpu.VMEM((second, everything), jnp.float32)] * 2
         + [pltpu.VMEM((full, full), jnp.float32)] * 2

time: 747 us -> 745 us (level)
  no operation moved by 1% of the time
where the time goes in v4:
time: 745 us; the launch traced here: 736 us
  Pallas kernels  735 us (99%)
    pallas_call x1, Pallas kernels, local(): pl.pallas_call(functools.partial(kernel, wide), out_shape=shapes, in_spec...  724 us

profile of v4, /device:TPU:1, one launch (start us, length us, event | category | flops | bytes accessed | tf_op | source)
XLA Modules:
  0.0 736.0 jit_solution(13054371271247091420)
XLA Ops:
  0.6 723.6 %shard_map.104 = (f32[64,128,256]{2,1,0:T(8,128)}, f32[64,128,256]{2,1,0:T(8,128)}, f32[64,128,256]{2,1,0:T(8,128)}, f32[64,128,256]{2,1,0:T(8,128)}, f32[64,128...) custom-call(f32[2,64,128,256]{3,2,1,0:T(8,128)} %wave.1, ...), custom_call_target="tpu_custom_call" | custom-call | flops 180388626432 | bytes 335544320 | tf_op jit(solution)/shard_map/pallas_call | solution.py:540
  724.3 11.7 %shard_map.105 = (f32[2,64,128,256]{3,2,1,0:T(8,128)}, f32[2,64,128,256]{3,2,1,0:T(8,128)}) custom-call(f32[4,64,128,256]{3,2,1,0:T(8,128)S(1)} %get-tuple-element.3.results), custom_call_target="tpu_custom_call" | custom-call | bytes 33554432 | tf_op jit(solution)/shard_map/pallas_call | solution.py:571

commit v5 on v4

--- a/solution.py
+++ b/solution.py
@@ -10,12 +10,13 @@
 half_step = 0.1
 MESH = pl.DeviceIdType.MESH
 OWN, END, FWD, YROW, WROW, PSI, PHI, SUM_O, SUM_F, YEND = range(10)
+late_rows = 4
 TO_S1, BACK_C, BACK_K, TO_S0, TO_W0, BACK_0 = range(6)
 BUFFERS = (
     "end0", "other0", "far0", "y0", "w0", "sy", "sw",
     "s0b", "t0", "w0b", "tw", "r0", "b0",
     "s1b", "t1", "rc", "rk", "bc", "bk", "phi",
-    "psie", "phie", "po", "pe", "ao", "af", "ba0", "ba1", "se", "y1", "s0", "s1",
+    "psie", "phie", "po", "pe", "ao", "af", "ba0", "ba1", "se", "y1", "s0", "s1", "late", "held",
 )
 WIDE_SHAPED = ("t0", "tw", "r0", "t1", "rc", "rk")
 SECOND_FIRST = ("s0b", "w0b", "b0", "s1b", "bc", "bk")
@@ -34,7 +35,7 @@
 def kernel(wide, wave, prev, pot, k2, c2, k1, c1, k3, c3, *refs):
     buf = dict(zip(BUFFERS, refs[:len(BUFFERS)]))
     (results, wh, wl, wth, wtl, k1h, k1l, c1h, c1l, k3h, k3l, c3h, c3l, fh, fl, gather, wend, land,
-     k2v, c2v, k1v, c1v, k3v, c3v, zs, zr, es, er, ms, ws, wr, wloc) = refs[len(BUFFERS):]
+     k2v, c2v, k1v, c1v, k3v, c3v, zs, zr, es, er, ms, ls, ws, wr, wloc) = refs[len(BUFFERS):]
     rows, second, third = wave.shape[1:]
     full = rows * wide
     q = second // wide
@@ -91,8 +92,18 @@
 
     def last_near():
         return pltpu.make_async_remote_copy(
-            src_ref=buf["ao"].at[pl.ds(rows - step, step)], dst_ref=land, send_sem=zs.at[SUM_O, nc - 1],
+            src_ref=buf["ao"].at[pl.ds(rows - step, step - late_rows)], dst_ref=land, send_sem=zs.at[SUM_O, nc - 1],
             recv_sem=zr.at[SUM_O, nc - 1], device_id={"narrow": other}, device_id_type=MESH)
+
+    def held_copies():
+        late = pl.ds(rows - late_rows, late_rows)
+        return [
+            pltpu.make_async_copy(slope.at[0, late], buf["held"].at[0], ls.at[1]),
+            pltpu.make_async_copy(following.at[0, late], buf["held"].at[1], ls.at[2]),
+        ]
+
+    def late_copy():
+        return pltpu.make_async_copy(buf["ao"].at[pl.ds(rows - late_rows, late_rows)], buf["late"], ls.at[0])
 
     def each_chunk(f):
         def body(c, carry):
@@ -410,6 +421,7 @@
             @pl.when(c == nc - 1)
             def _():
                 last_near().start()
+                late_copy().start()
 
             @pl.when(c < nc - 2)
             def _():
@@ -444,6 +456,8 @@
             @pl.when(c == nc - 1)
             def _():
                 own_sum_stage(c, "po")
+                for copy in held_copies():
+                    copy.start()
 
         @pl.when(t == base_at)
         def _():
@@ -489,8 +503,11 @@
             def _():
                 zsent(SUM_O, c, buf["ao"])
         each_chunk(sent)
+        late_copy().wait()
+        for copy in held_copies():
+            copy.wait()
         last_near().wait_recv()
-        tail = slice(rows - step, rows)
+        tail = slice(rows - step, rows - late_rows)
         value = land[...]
         results[0, tail] = results[0, tail] + value
         results[2, tail] = results[2, tail] + half_step * value
@@ -505,14 +522,36 @@
             zrecv(YEND, c, buf["y1"])
             own_sum_stage(c, "y1")
         each_chunk(sent)
+        for copy in held_copies():
+            copy.start()
         for n, matrix in enumerate((k2, c2)):
             end_matrix(n, matrix).wait_send()
+        for copy in held_copies():
+            copy.wait()
 
 
 def write_kernel(results, slope_out, following_out, sems):
+    ready = pl.ds(0, results.shape[1] - late_rows)
     copies = [
-        pltpu.make_async_copy(results.at[pl.ds(0, 2)], slope_out, sems.at[0]),
-        pltpu.make_async_copy(results.at[pl.ds(2, 2)], following_out, sems.at[1]),
+        pltpu.make_async_copy(results.at[0, ready], slope_out.at[0, ready], sems.at[0]),
+        pltpu.make_async_copy(results.at[1], slope_out.at[1], sems.at[1]),
+        pltpu.make_async_copy(results.at[2, ready], following_out.at[0, ready], sems.at[2]),
+        pltpu.make_async_copy(results.at[3], following_out.at[1], sems.at[3]),
+    ]
+    for copy in copies:
+        copy.start()
+    for copy in copies:
+        copy.wait()
+
+
+def late_kernel(base, came, slope_in, following_in, slope_out, following_out, held, sems):
+    at = pl.ds(slope_out.shape[1] - late_rows, late_rows)
+    value = came[...]
+    held[0] = base[0] + value
+    held[1] = base[1] + half_step * value
+    copies = [
+        pltpu.make_async_copy(held.at[0], slope_out.at[0, at], sems.at[0]),
+        pltpu.make_async_copy(held.at[1], following_out.at[0, at], sems.at[1]),
     ]
     for copy in copies:
         copy.start()
@@ -526,7 +565,11 @@
     q = second // wide
     shapes = []
     for name in BUFFERS:
-        if name in WIDE_SHAPED:
+        if name == "late":
+            shape = (late_rows, second, third)
+        elif name == "held":
+            shape = (2, late_rows, second, third)
+        elif name in WIDE_SHAPED:
             shape = (q, full, third)
         elif name in SECOND_FIRST:
             shape = (second, rows, third)
@@ -550,7 +593,7 @@
             pltpu.VMEM((everything, third), bf),
             pltpu.VMEM((4, second, third), jnp.float32),
             pltpu.VMEM((2, second, everything), jnp.float32),
-            pltpu.VMEM((8, second, third), jnp.float32),
+            pltpu.VMEM((8 - late_rows, second, third), jnp.float32),
         ]
         + [pltpu.VMEM((second, everything), jnp.float32)] * 2
         + [pltpu.VMEM((full, full), jnp.float32)] * 2
@@ -561,6 +604,7 @@
             pltpu.SemaphoreType.DMA((2,)),
             pltpu.SemaphoreType.DMA((2,)),
             pltpu.SemaphoreType.DMA((6,)),
+            pltpu.SemaphoreType.DMA((3,)),
             pltpu.SemaphoreType.DMA((6,)),
             pltpu.SemaphoreType.DMA((6,)),
             pltpu.SemaphoreType.DMA((6,)),
@@ -568,15 +612,29 @@
         compiler_params=pltpu.CompilerParams(collective_id=0, has_side_effects=True, vmem_limit_bytes=26 * 2**20),
         cost_estimate=pl.CostEstimate(flops=6 * 3584 * 2 * rows * second * third * 2, bytes_accessed=40 * rows * second * third * 4, transcendentals=0),
     )(wavefunction, previous_slope, potential, kinetic_two, coupling_two, kinetic_one, coupling_one, kinetic_three, coupling_three)
-    return pl.pallas_call(
+    results = outs[len(BUFFERS)]
+    came = lax.ppermute(outs[BUFFERS.index("late")], "narrow", [(1, 2), (2, 1)])
+    shapes = [jax.ShapeDtypeStruct(wavefunction.shape, jnp.float32)] * 2
+    whole = [pl.BlockSpec(memory_space=pl.ANY)] * 2
+    written = pl.pallas_call(
         write_kernel,
         in_specs=[pl.BlockSpec(memory_space=pltpu.VMEM)],
-        out_specs=[pl.BlockSpec(memory_space=pl.ANY)] * 2,
-        out_shape=[jax.ShapeDtypeStruct(wavefunction.shape, jnp.float32)] * 2,
-        scratch_shapes=[pltpu.SemaphoreType.DMA((2,))],
+        out_specs=whole,
+        out_shape=shapes,
+        scratch_shapes=[pltpu.SemaphoreType.DMA((4,))],
         compiler_params=pltpu.CompilerParams(vmem_limit_bytes=2**20),
         cost_estimate=pl.CostEstimate(flops=0, bytes_accessed=wavefunction.size * 8, transcendentals=0),
-    )(*outs[len(BUFFERS):])
+    )(results)
+    return pl.pallas_call(
+        late_kernel,
+        in_specs=[pl.BlockSpec(memory_space=pltpu.VMEM)] * 2 + whole,
+        out_specs=whole,
+        out_shape=shapes,
+        input_output_aliases={2: 0, 3: 1},
+        scratch_shapes=[pltpu.VMEM((2, late_rows, second, third), jnp.float32), pltpu.SemaphoreType.DMA((2,))],
+        compiler_params=pltpu.CompilerParams(vmem_limit_bytes=4 * 2**20),
+        cost_estimate=pl.CostEstimate(flops=0, bytes_accessed=late_rows * second * third * 12, transcendentals=0),
+    )(outs[BUFFERS.index("held")], came, *written)
 
 
 def solution(mesh):

time: 745 us -> 744 us (level)
  transfers between devices with their start and end apart: 0 -> 1, of which waited for: 0 -> 0; matrix products, arithmetic and copies ran while one was open for 0% -> 0% of each run, Pallas kernels for 0% -> 1%
where the time goes in v5:
time: 744 us; the launch traced here: 738 us
  Pallas kernels  737 us (99%)
    pallas_call x1, Pallas kernels, local(): pl.pallas_call(functools.partial(kernel, wide), out_shape=shapes, in_spec...  725 us
  transfers between devices with their start and end apart: 1, of which 0 were waited for; matrix products, arithmetic and copies ran while one was open for 0% of the time, Pallas kernels for 1%

profile of v5, /device:TPU:1, one launch (start us, length us, event | category | flops | bytes accessed | tf_op | source)
XLA Modules:
  0.0 738.1 jit_solution(9609294521455587907)
XLA Ops:
  0.6 724.7 %shard_map.104 = (f32[64,128,256]{2,1,0:T(8,128)}, f32[64,128,256]{2,1,0:T(8,128)}, f32[64,128,256]{2,1,0:T(8,128)}, f32[64,128,256]{2,1,0:T(8,128)}, f32[64,128...) custom-call(f32[2,64,128,256]{3,2,1,0:T(8,128)} %wave.1, ...), custom_call_target="tpu_custom_call" | custom-call | flops 180388626432 | bytes 335544320 | tf_op jit(solution)/shard_map/pallas_call | solution.py:583
  725.3 0.7 collective-permute-start
  726.0 0.0 copy-start
  726.1 10.9 %shard_map.105 = (f32[2,64,128,256]{3,2,1,0:T(8,128)}, f32[2,64,128,256]{3,2,1,0:T(8,128)}) custom-call(f32[4,64,128,256]{3,2,1,0:T(8,128)S(1)} %get-tuple-element.9.results), custom_call_target="tpu_custom_call" | custom-call | bytes 33554432 | tf_op jit(solution)/shard_map/pallas_call | solution.py:619
  737.0 0.0 collective-permute-done.came
  737.0 0.0 copy-done
  737.0 1.1 shard_map.106
Async XLA Ops:
  725.3 11.6 %collective-permute-start = (f32[4,128,256]{2,1,0:T(8,128)}, f32[4,128,256]{2,1,0:T(8,128)S(1)}, u32[]{:S(2)}, u32[]{:S(2)}) collective-permute-start(f32[4,128,256]{2,1,0:T(8,128)} %get-tuple-element.8), channel_id=1, source_target_pairs={{1,2},{2,1},{5,6},{6,5},{9,10},{10,9},{13,14},{14,13},{17,18},{18,... | collective-permute-start | bytes 1572872 | tf_op jit(solution)/shard_map/ppermute | solution.py:616
  726.0 10.9 %copy-start = (f32[2,4,128,256]{3,2,1,0:T(8,128)S(1)}, f32[2,4,128,256]{3,2,1,0:T(8,128)}, u32[]{:S(2)}) copy-start(f32[2,4,128,256]{3,2,1,0:T(8,128)} %get-tuple-element.7.base) | copy-start | bytes 3145732

commit v6 on v5

--- a/solution.py
+++ b/solution.py
@@ -414,12 +414,7 @@
             scatter_stage(c)
             zcopy(SUM_F, c, buf["af"], buf["ba1"], other).start()
 
-            @pl.when(jnp.logical_and(c == nc - 1, nc > 1))
-            def _():
-                zcopy(SUM_O, max(nc - 2, 0), buf["ao"], buf["ba0"], other).start()
-
-            @pl.when(c == nc - 1)
-            def _():
+            if nc == 1:
                 last_near().start()
                 late_copy().start()
 
@@ -446,7 +441,16 @@
                 end_sum_stage(e)
                 zcopy(YEND, e, buf["se"], buf["y1"], end).start()
                 return carry
+
+            @pl.when(c == nc - 2)
+            def _():
+                zcopy(SUM_O, c, buf["ao"], buf["ba0"], other).start()
             lax.fori_loop(c, c + here, far_sum, 0)
+
+            @pl.when(c == nc - 2)
+            def _():
+                last_near().start()
+                late_copy().start()
 
             @pl.when(c < nc - 1)
             def _():

time: 744 us -> 743 us (level)
  no operation moved by 1% of the time
where the time goes in v6:
time: 743 us; the launch traced here: 737 us
  Pallas kernels  736 us (99%)
    pallas_call x1, Pallas kernels, local(): pl.pallas_call(functools.partial(kernel, wide), out_shape=shapes, in_spec...  724 us
  transfers between devices with their start and end apart: 1, of which 0 were waited for; matrix products, arithmetic and copies ran while one was open for 0% of the time, Pallas kernels for 1%

profile of v6, /device:TPU:1, one launch (start us, length us, event | category | flops | bytes accessed | tf_op | source)
XLA Modules:
  0.0 737.3 jit_solution(14134109493827809244)
XLA Ops:
  0.6 723.9 %shard_map.104 = (f32[64,128,256]{2,1,0:T(8,128)}, f32[64,128,256]{2,1,0:T(8,128)}, f32[64,128,256]{2,1,0:T(8,128)}, f32[64,128,256]{2,1,0:T(8,128)}, f32[64,128...) custom-call(f32[2,64,128,256]{3,2,1,0:T(8,128)} %wave.1, ...), custom_call_target="tpu_custom_call" | custom-call | flops 180388626432 | bytes 335544320 | tf_op jit(solution)/shard_map/pallas_call | solution.py:587
  724.5 0.7 collective-permute-start
  725.2 0.0 copy-start
  725.3 10.9 %shard_map.105 = (f32[2,64,128,256]{3,2,1,0:T(8,128)}, f32[2,64,128,256]{3,2,1,0:T(8,128)}) custom-call(f32[4,64,128,256]{3,2,1,0:T(8,128)S(1)} %get-tuple-element.9.results), custom_call_target="tpu_custom_call" | custom-call | bytes 33554432 | tf_op jit(solution)/shard_map/pallas_call | solution.py:623
  736.2 0.0 collective-permute-done.came
  736.2 0.0 copy-done
  736.2 1.1 shard_map.106
Async XLA Ops:
  724.5 11.6 %collective-permute-start = (f32[4,128,256]{2,1,0:T(8,128)}, f32[4,128,256]{2,1,0:T(8,128)S(1)}, u32[]{:S(2)}, u32[]{:S(2)}) collective-permute-start(f32[4,128,256]{2,1,0:T(8,128)} %get-tuple-element.8), channel_id=1, source_target_pairs={{1,2},{2,1},{5,6},{6,5},{9,10},{10,9},{13,14},{14,13},{17,18},{18,... | collective-permute-start | bytes 1572872 | tf_op jit(solution)/shard_map/ppermute | solution.py:620
  725.2 10.9 %copy-start = (f32[2,4,128,256]{3,2,1,0:T(8,128)S(1)}, f32[2,4,128,256]{3,2,1,0:T(8,128)}, u32[]{:S(2)}) copy-start(f32[2,4,128,256]{3,2,1,0:T(8,128)} %get-tuple-element.7.base) | copy-start | bytes 3145732
